TPU v7x, 512 devices: a whole 4x8x8 slice. The times are simulated.
512 devices in a mesh: group: 8 (over x, z_hi), dev: 64 (over y, z_lo, core).
Axes of the slice: x: 4, y: 8, z: 8 (z_hi: 2, z_lo: 4; z = z_hi * 4 + z_lo), core: 2. Of those that a mesh axis runs over, the one named last changes fastest.
Arguments:
- tokens: bfloat16 [8192, 8192], P(('group', 'dev'))
- query_grad: bfloat16 [8192, 8192], P(('group', 'dev')), may hold values from -0.06591797 to 0.06591797
- gain: float32 [8192], replicated, may hold values from 0.1 to 1.9
- master: float32 [64, 8, 8, 16384], P('dev', 'group'), may hold values from -6 to 6
- momentum: float32 [64, 8, 8, 16384], P('dev', 'group'), may hold values from -6 to 6
- owner: int32 [64, 64], replicated, may hold values from 0 to 7, as said below
Outputs:
- master_new: float32 [64, 8, 8, 16384], P('dev', 'group')
- momentum_new: float32 [64, 8, 8, 16384], P('dev', 'group')
- params_new: bfloat16 [8192, 8192], P(None, 'dev')
Inputs may be any that keep to these rules, and one draw needn't show every extreme that they name: `owner`: for every column block d, each group owns exactly 8 of its 64 partitions.
All inputs are finite; a program needn't handle non-finite values.
Results may differ from a plain program's by a relative error of at most 0.013.
Values may be sent and summed in bfloat16 or wider, within the bound.
No kernel may reach another device: no remote copies, remote signals or barrier semaphores. Data moves between devices by JAX's collectives and lax.ppermute only.
A program may use at most 128 MiB of HBM per device.

v0:
```python
import jax
import jax.numpy as jnp
from jax import lax
from jax.sharding import PartitionSpec as P

norm_eps = 1e-05
momentum_rate = 0.9
learn_rate = 0.2


def slot_table(owner_row, groups):
    part_count = owner_row.shape[0]
    per_group = part_count // groups
    onehot = (owner_row[:, None] == jnp.arange(groups, dtype=jnp.int32)[None, :]).astype(jnp.int32)
    before = jnp.cumsum(onehot, axis=0) - onehot
    rank_in = jnp.sum(before * onehot, axis=1)
    slot_of = owner_row * per_group + rank_in
    places = jnp.arange(part_count, dtype=jnp.int32)
    source = jnp.sum(jnp.where(slot_of[None, :] == places[:, None], places[None, :], 0), axis=1)
    return (slot_of, source)


def local(tokens, query_grad, gain, master, momentum, owner):
    groups = lax.axis_size("group")
    devices = lax.axis_size("dev")
    model_width = tokens.shape[1]
    columns = model_width // devices
    part_size = master.shape[-1]
    part_count = owner.shape[1]
    owner_row = lax.dynamic_slice_in_dim(owner, lax.axis_index("dev"), 1, 0)[0]
    slot_of, source = slot_table(owner_row, groups)
    values = tokens.astype(jnp.float32)
    mean_square = jnp.mean(values * values, axis=1, keepdims=True)
    normed = (values * lax.rsqrt(mean_square + norm_eps) * gain[None, :]).astype(jnp.bfloat16)
    cotangent = lax.all_to_all(query_grad, "dev", split_axis=1, concat_axis=0, tiled=True)
    gradient = lax.dot_general(
        lax.all_gather(normed, "dev", axis=0, tiled=True),
        cotangent,
        (((0,), (0,)), ((), ())),
        preferred_element_type=jnp.float32,
    )
    packed = jnp.take(gradient.reshape(part_count, part_size), source, axis=0)
    summed = lax.psum_scatter(
        packed.astype(jnp.bfloat16), "group", scatter_dimension=0, tiled=True
    ).astype(jnp.float32)
    momentum_new = momentum_rate * momentum[0, 0] + summed
    master_new = master[0, 0] - learn_rate * momentum_new
    pulled = lax.all_gather(master_new.astype(jnp.bfloat16), "group", axis=0, tiled=True)
    params_new = jnp.take(pulled, slot_of, axis=0).reshape(model_width, columns)
    return (master_new[None, None], momentum_new[None, None], params_new)


def solution(mesh):
    placed = (
        P(("group", "dev"), None),
        P(("group", "dev"), None),
        P(),
        P("dev", "group", None, None),
        P("dev", "group", None, None),
        P(),
    )
    return jax.shard_map(
        local,
        mesh=mesh,
        in_specs=placed,
        out_specs=(P("dev", "group", None, None), P("dev", "group", None, None), P(None, "dev")),
        check_vma=False,
    )
```

profile of v0, /device:TPU:1, one launch (start us, length us, event | category | flops | bytes accessed | tf_op | source)
XLA Modules:
  0.0 373.9 jit_solution(1405405721456284469)
XLA Ops:
  7.2 0.0 copy-start
  7.2 0.0 all-gather.3.cloned.1.call-start
  7.2 1.2 fusion
  8.4 1.8 fusion.2
  10.2 0.0 all-gather.3.cloned.1.call-update
  10.2 0.0 copy-done
  10.2 0.7 copy_bitcast_fusion
  11.0 14.6 %all-to-all-start = ((bf16[16,64,128]{2,0,1:T(8,128)(2,1)}), bf16[16,64,128]{2,0,1:T(8,128)(2,1)S(1)}, u32[]{:S(2)}, u32[]{:S(2)}) async-start(bf16[16,64,128]{2,0,1:T(8,128)(2,1)} %copy_bitcast_fusion), calls=%async_computation | async-start | bytes 524288 | tf_op jit(solution)/shard_map/all_to_all | solution.py:35
  25.6 0.0 reduce-scatter.2.cloned.1.call-start
  25.6 0.7 fusion.13
  26.3 0.1 fusion.4
  26.4 0.1 reduce_window_sum.11
  26.5 0.2 select_reduce_fusion.1
  26.7 0.7 fusion.9
  27.4 0.1 select_reduce_fusion
  27.5 10.6 %all-to-all-done = bf16[16,64,128]{2,0,1:T(8,128)(2,1)S(1)} async-done(((bf16[16,64,128]{2,0,1:T(8,128)(2,1)}), bf16[16,64,128]{2,0,1:T(8,128)(2,1)S(1)}, u32[]{:S(2)}, u32[]{:S(2)}) %all-to-all-start) | async-done | bytes 262176 | tf_op jit(solution)/shard_map/all_to_all | solution.py:35
  38.1 115.1 %all-gather.3.cloned.1.call-done = bf16[1024,8192]{1,0:T(8,128)(2,1)} async-done(((bf16[16,8192]{1,0:T(8,128)(2,1)}), bf16[1024,8192]{1,0:T(8,128)(2,1)}) %all-gather.3.cloned.1.call-update) | async-done | bytes 16777232 | tf_op jit(solution)/shard_map/all_gather | solution.py:37
  153.2 9.6 %fusion.10 = bf16[8192,128]{1,0:T(8,128)(2,1)} fusion(bf16[1024,8192]{1,0:T(8,128)(2,1)} %all-gather.3.cloned.1.call-done, bf16[1024,128]{1,0:T(8,128)(2,1)S(1)} %bitcast.53), kind=kOutput, calls=%fused_computation.36 | convolution fusion | flops 2147483648 | bytes 19136512 | tf_op jit(solution)/shard_map/dot_general | solution.py:36
  162.9 2.8 reshape.81
  165.7 3.2 gather_fusion
  168.9 3.3 select_convert_fusion
  172.2 0.0 copy-start.1
  172.2 0.0 copy-start.2
  172.2 0.0 reduce-scatter.2.cloned.1.call-update
  172.2 0.0 all-gather.5.cloned.1.call-start
  172.3 98.3 %reduce-scatter.2.cloned.1.call-done = bf16[8,16384]{1,0:T(8,128)(2,1)} async-done(((bf16[64,16384]{1,0:T(8,128)(2,1)}), bf16[8,16384]{1,0:T(8,128)(2,1)}) %reduce-scatter.2.cloned.1.call-update) | async-done | bytes 262160 | tf_op jit(solution)/shard_map/reduce_scatter | solution.py:43
  270.5 0.0 copy-done.1
  270.5 0.0 copy-done.2
  270.5 2.1 fusion.5
  272.6 0.0 all-gather.5.cloned.1.call-update
  272.7 0.7 fusion.8
  273.4 0.7 compare_and_fusion
  274.1 0.1 broadcast_bitcast_fusion
  274.2 78.4 %all-gather.5.cloned.1.call-done = bf16[64,16384]{1,0:T(8,128)(2,1)} async-done(((bf16[8,16384]{1,0:T(8,128)(2,1)}), bf16[64,16384]{1,0:T(8,128)(2,1)}) %all-gather.5.cloned.1.call-update) | async-done | bytes 2097168 | tf_op jit(solution)/shard_map/all_gather | solution.py:48
  352.6 6.9 %gather_fusion.1 = bf16[64,16384]{1,0:T(8,128)(2,1)} fusion(bf16[64,16384]{1,0:T(8,128)(2,1)} %all-gather.5.cloned.1.call-done, s32[1024]{0:T(1024)S(1)} %pad_clamp_fusion), kind=kCustom, calls=%fused_computation.1 | custom fusion | bytes 4194560 | tf_op jit(solution)/shard_map/jit(_take)/gather | solution.py:49
  359.5 2.9 gather.12
  362.3 5.0 %broadcast_select_fusion = bf16[8192,128]{1,0:T(8,128)(2,1)} fusion(bf16[8192,128]{1,0:T(8,128)(2,1)S(1)} %gather.12, pred[8192]{0:T(1024)(128)(4,1)S(1)} %broadcast_bitcast_fusion), kind=kLoop, calls=%fused_computation.3 | loop fusion | flops 1048576 | bytes 4202496 | tf_op jit(solution)/shard_map/jit(_take)/select_n | solution.py:49
  (5 shorter events, 0.0 us)
Async XLA Ops:
  7.2 3.1 copy-start
  7.2 146.0 %all-gather.3.cloned.1.call-start = ((), (), s32[]{:S(2)}) async-start(), calls=%async_computation.2 | async-start | bytes 17039360 | tf_op jit(solution)/shard_map/all_gather | solution.py:37
  11.0 27.2 %all-to-all-start = ((bf16[16,64,128]{2,0,1:T(8,128)(2,1)}), bf16[16,64,128]{2,0,1:T(8,128)(2,1)S(1)}, u32[]{:S(2)}, u32[]{:S(2)}) async-start(bf16[16,64,128]{2,0,1:T(8,128)(2,1)} %copy_bitcast_fusion), calls=%async_computation | async-start | bytes 524288 | tf_op jit(solution)/shard_map/all_to_all | solution.py:35
  25.6 245.0 %reduce-scatter.2.cloned.1.call-start = ((), (), s32[]{:S(2)}) async-start(), calls=%async_computation.3 | async-start | bytes 2359296 | tf_op jit(solution)/shard_map/reduce_scatter | solution.py:43
  172.2 98.3 %copy-start.1 = (f32[1,1,8,16384]{3,2,1,0:T(8,128)S(1)}, f32[1,1,8,16384]{3,2,1,0:T(8,128)}, u32[]{:S(2)}) copy-start(f32[1,1,8,16384]{3,2,1,0:T(8,128)} %param.10) | copy-start | bytes 1572868
  172.2 98.3 %copy-start.2 = (f32[1,1,8,16384]{3,2,1,0:T(8,128)S(1)}, f32[1,1,8,16384]{3,2,1,0:T(8,128)}, u32[]{:S(2)}) copy-start(f32[1,1,8,16384]{3,2,1,0:T(8,128)} %param.9) | copy-start | bytes 1572868
  172.2 180.4 %all-gather.5.cloned.1.call-start = ((), (), s32[]{:S(2)}) async-start(), calls=%async_computation.4 | async-start | bytes 2359296 | tf_op jit(solution)/shard_map/all_gather | solution.py:48
Sparse Core Ops, SparseCore 0:
  10.7 142.4 all-gather.2
  172.4 98.1 reduce-scatter.1
  274.8 77.7 all-gather.4
where the time goes:
time: 375 us; the launch traced here: 374 us
  waiting for transfers between devices  302 us (81%)
  local copies, waits for them, and re-layouts  17.3 us (5%)
  other arithmetic  16 us (4%)
  starting transfers between devices  14.7 us (4%)
  between operations  13.8 us (4%)
  matrix products  9.65 us (3%)
    all_gather x1, waiting for transfers between devices, local(): lax.all_gather(normed, 'dev', axis=0, tiled=True)  115 us
    reduce_scatter x1, waiting for transfers between devices, local(): lax.psum_scatter(packed.astype(jnp.bfloat16), 'group', scatter_dimension=...  98.3 us
    all_gather x1, waiting for transfers between devices, local(): lax.all_gather(master_new.astype(jnp.bfloat16), 'group', axis=0, tiled=True)  78.4 us
    all_to_all x1, starting transfers between devices, local(): lax.all_to_all(query_grad, 'dev', split_axis=1, concat_axis=0, tiled=True)  14.6 us
    all_to_all x1, waiting for transfers between devices, local(): lax.all_to_all(query_grad, 'dev', split_axis=1, concat_axis=0, tiled=True)  10.6 us
    gather x2, local copies, waits for them, and re-layouts, local(): params_new = jnp.take(pulled, slot_of, axis=0).reshape(model_width, columns)  9.74 us
    dot_general x1, matrix products, local(): lax.dot_general(lax.all_gather(normed, 'dev', axis=0, tiled=True), cotang...  9.65 us
  transfers between devices with their start and end apart: 4, of which 4 were waited for; matrix products, arithmetic and copies ran while one was open for 1% of the time, Pallas kernels for 0%

commit v1 on v0

v1 whole, which is shorter than its diff:
```python
import functools

import jax
import jax.numpy as jnp
from jax import lax
from jax.experimental import pallas as pl
from jax.experimental.pallas import tpu as pltpu
from jax.sharding import Mesh, PartitionSpec as P

norm_eps = 1e-05
momentum_rate = 0.9
learn_rate = 0.2

PARTS = (("x", 4), ("h", 2), ("y", 8), ("l", 4), ("c", 2))
GROUP = ("x", "h")
DEV = ("y", "l", "c")


def slot_table(owner_row, groups):
    onehot = (owner_row[:, None] == jnp.arange(groups, dtype=jnp.int32)[None, :]).astype(jnp.int32)
    before = jnp.cumsum(onehot, axis=0) - onehot
    return jnp.sum(before * onehot, axis=1)


def spread_x(block):
    return lax.all_to_all(
        jnp.broadcast_to(block[None], (lax.axis_size("x"), *block.shape)), "x", split_axis=0, concat_axis=0, tiled=True
    )


def swap(block, axis):
    return lax.ppermute(block, axis, [(0, 1), (1, 0)])


def finish_kernel(per_group, part_rows, h_ref, source_ref, place_ref, own_ref, other_ref, pulled_ref, master_ref,
                  momentum_ref, master_out, momentum_out, params_out, work_ref):
    a = pl.program_id(0)
    h = h_ref[0]
    columns = params_out.shape[1]
    x = lax.div(a, 2)
    in_own = lax.rem(a, 2) == h
    for p in range(per_group):
        rows = pl.ds(p * part_rows, part_rows)
        held = pulled_ref[place_ref[a * per_group + p]].astype(jnp.float32)

        @pl.when(in_own)
        def _(rows=rows, held=held):
            params_out[rows, :] = (held - learn_rate * own_ref[x, rows, :].astype(jnp.float32)).astype(jnp.bfloat16)

        @pl.when(jnp.logical_not(in_own))
        def _(rows=rows, held=held):
            params_out[rows, :] = (held - learn_rate * other_ref[x, rows, :].astype(jnp.float32)).astype(jnp.bfloat16)

    step = master_ref.shape[1] // columns
    for j in range(per_group):
        k = source_ref[j]
        block = lax.div(k, per_group)
        start = pl.multiple_of(lax.rem(k, per_group) * part_rows + a * step, step)
        bx = lax.div(block, 2)
        mine = own_ref[bx, pl.ds(start, step), :].astype(jnp.float32)
        theirs = other_ref[bx, pl.ds(start, step), :].astype(jnp.float32)
        work_ref[pl.ds(j * step, step), :] = jnp.where(lax.rem(block, 2) == h, mine, theirs)
    for r in range(step):
        grad = work_ref[pl.ds(r, per_group, stride=step), :]
        cols = pl.ds(r * columns, columns)
        momentum_new = momentum_rate * momentum_ref[:, cols] + grad
        momentum_out[:, cols] = momentum_new
        master_out[:, cols] = master_ref[:, cols] - learn_rate * momentum_new


def finish(h, source, place, own, other, pulled, master, momentum):
    nx, rows, columns = own.shape
    part_count, part_rows, _ = pulled.shape
    per_group, part_size = master.shape
    groups = part_count // per_group
    whole = lambda arr: pl.BlockSpec(arr.shape, lambda a, *_: (0,) * arr.ndim)
    served = pl.BlockSpec((per_group, part_size // groups), lambda a, *_: (0, a))
    return pl.pallas_call(
        functools.partial(finish_kernel, per_group, part_rows),
        grid_spec=pltpu.PrefetchScalarGridSpec(
            num_scalar_prefetch=3,
            grid=(groups,),
            in_specs=[whole(own), whole(other), whole(pulled), served, served],
            out_specs=[served, served, pl.BlockSpec((rows, columns), lambda a, *_: (a, 0))],
            scratch_shapes=[pltpu.VMEM((per_group * part_rows // groups, columns), jnp.float32)],
        ),
        out_shape=[
            jax.ShapeDtypeStruct(master.shape, jnp.float32),
            jax.ShapeDtypeStruct(master.shape, jnp.float32),
            jax.ShapeDtypeStruct((groups * rows, columns), jnp.bfloat16),
        ],
        compiler_params=pltpu.CompilerParams(vmem_limit_bytes=24 * 1024 * 1024),
        cost_estimate=pl.CostEstimate(flops=4_000_000, bytes_accessed=8_000_000, transcendentals=0),
        name="finish",
    )(h.reshape(1), source, place, own, other, pulled, master, momentum)


def local(tokens, query_grad, gain, master, momentum, owner):
    nx, nh, ny, nl, nc = (lax.axis_size(name) for name, _ in PARTS)
    groups = nx * nh
    own, width = tokens.shape
    columns = width // (ny * nl * nc)
    rows = width // groups
    part_size = master.shape[-1]
    part_count = owner.shape[1]
    per_group = part_count // groups
    part_rows = part_size // columns
    h = lax.axis_index("h")
    c = lax.axis_index("c")
    me = lax.axis_index(GROUP)

    sent = tokens.reshape(own, nx, nh, rows)
    sent = jnp.concatenate(
        [jnp.where(h == 0, sent[:, :, 0], sent[:, :, 1]), jnp.where(h == 0, sent[:, :, 1], sent[:, :, 0])], axis=0
    )
    sent = sent.transpose(1, 0, 2)
    mine = lax.all_to_all(sent, "x", split_axis=0, concat_axis=0, tiled=True)
    pair = jnp.stack([mine[:, :own], swap(mine[:, own:], "h")])
    left = lax.all_gather(pair, "y", axis=0, tiled=False)

    values = tokens.astype(jnp.float32)
    scale = lax.rsqrt(jnp.mean(values * values, axis=1, keepdims=True) + norm_eps)
    scaled = (query_grad.astype(jnp.float32) * scale).astype(jnp.bfloat16)
    scaled = scaled.reshape(own, ny, nl, nc, columns)
    scaled = jnp.where(c == 0, scaled[:, :, :, ::-1], scaled)
    scaled = scaled.transpose(1, 0, 3, 2, 4).reshape(ny, own, nc * nl * columns)
    part = lax.all_to_all(scaled, "y", split_axis=0, concat_axis=0, tiled=True)
    part_other = swap(part, "h")
    right_own = spread_x(part)
    right_own, part_other = lax.optimization_barrier((right_own, part_other))
    right_other = spread_x(part_other)
    right = jnp.concatenate([right_own, right_other], axis=0)

    before = (master[0, 0] - learn_rate * momentum_rate * momentum[0, 0]).astype(jnp.bfloat16)
    before = before.reshape(per_group, part_rows, columns)
    before, _ = lax.optimization_barrier((before, part_other))
    pair = jnp.stack([before, swap(before, "h")], axis=0)
    pulled = lax.all_gather(pair, "x", axis=0, tiled=False)
    pulled = pulled.reshape(part_count, part_rows, columns)
    owner_row = lax.dynamic_slice_in_dim(owner, lax.axis_index(DEV), 1, 0)[0]
    rank = slot_table(owner_row, groups)
    place = ((owner_row // nh) * nh + jnp.where(owner_row % nh == h, 0, 1)) * per_group + rank
    slots = jnp.arange(per_group, dtype=jnp.int32)
    hit = (owner_row[None, :] == me) & (rank[None, :] == slots[:, None])
    source = jnp.sum(jnp.where(hit, jnp.arange(part_count, dtype=jnp.int32)[None, :], 0), axis=1)

    weight = lax.dynamic_slice_in_dim(gain, me * rows, rows, 0)[:, None]

    def product(half):
        both = right[:, :, :, half * nl * columns : (half + 1) * nl * columns]
        both = both.transpose(1, 0, 2, 3).reshape(-1, nl * columns)
        return weight * lax.dot_general(
            left.reshape(-1, rows), both, (((0,), (0,)), ((), ())), preferred_element_type=jnp.float32
        )

    came = swap(product(0).astype(jnp.bfloat16), "c")
    both = (product(1) + came.astype(jnp.float32)).astype(jnp.bfloat16)
    both = both.reshape(rows, nl, columns).transpose(1, 0, 2)
    got = lax.all_to_all(both, "l", split_axis=0, concat_axis=0, tiled=True)
    summed = jnp.sum(got.astype(jnp.float32), axis=0).astype(jnp.bfloat16)
    summed, pulled, place, source = lax.optimization_barrier((summed, pulled, place, source))

    summed_other = swap(summed, "h")
    full_own = spread_x(summed)
    full_own, summed_other = lax.optimization_barrier((full_own, summed_other))
    full_other = spread_x(summed_other)
    master_new, momentum_new, params_new = finish(
        h, source, place, full_own, full_other, pulled, master[0, 0], momentum[0, 0]
    )
    return (master_new[None, None], momentum_new[None, None], params_new)


def solution(mesh):
    fine = Mesh(mesh.devices.reshape([size for _, size in PARTS]), [name for name, _ in PARTS])
    whole = (*GROUP, *DEV)
    server = P(DEV, GROUP, None, None)
    return jax.shard_map(
        local,
        mesh=fine,
        in_specs=(P(whole, None), P(whole, None), P(), server, server, P()),
        out_specs=(server, server, P(None, DEV)),
        check_vma=False,
    )
```

time: 375 us -> 199 us (0.53)
  waiting for transfers between devices: 302 us -> 52.5 us
  starting transfers between devices: 14.7 us -> 68.5 us
  blocking collectives: 0 us -> 33.2 us
  other arithmetic: 16 us -> 6.44 us
  local copies, waits for them, and re-layouts: 17.3 us -> 11.2 us
  Pallas kernels: 0 us -> 4.83 us
  matrix products: 9.65 us -> 5.28 us
    all_gather x2, waiting for transfers between devices: 194 us -> 0.04 us  [the longest x1 0.02 us: local(): left = lax.all_gather(pair, 'y', axis=0, tiled=False)]
    reduce_scatter x1 -> x0, waiting for transfers between devices: 98.3 us -> none  [local(): lax.psum_scatter(packed.astype(jnp.bfloat16), 'group', scatter_dimension=...]
    ppermute x0 -> x5, starting transfers between devices: none -> 47.8 us  [swap(): return lax.ppermute(block, axis, [(0, 1), (1, 0)])]
    all_to_all x0 -> x2, blocking collectives: none -> 33.2 us  [the longest x1 17.1 us: spread_x(): lax.all_to_all(jnp.broadcast_to(block[None], (lax.axis_size('x'), *block....]
    ppermute x0 -> x5, waiting for transfers between devices: none -> 24.3 us  [swap(): return lax.ppermute(block, axis, [(0, 1), (1, 0)])]
    all_to_all x1 -> x5, waiting for transfers between devices: 10.6 us -> 28.2 us  [the longest x1 22.9 us: local(): got = lax.all_to_all(both, 'l', split_axis=0, concat_axis=0, tiled=True)]
    gather x3 -> x0, local copies, waits for them, and re-layouts: 12.9 us -> none  [the longest x2 9.74 us: local(): params_new = jnp.take(pulled, slot_of, axis=0).reshape(model_width, columns)]
    convert_element_type x3 -> x1, other arithmetic: 7.21 us -> 0.12 us  [local(): scaled = (query_grad.astype(jnp.float32) * scale).astype(jnp.bfloat16)]
  transfers between devices with their start and end apart: 4 -> 12, of which waited for: 4 -> 7; matrix products, arithmetic and copies ran while one was open for 1% -> 9% of each run, Pallas kernels for 0% -> 0%
where the time goes in v1:
time: 199 us; the launch traced here: 196 us
  starting transfers between devices  68.5 us (34%)
  waiting for transfers between devices  52.5 us (26%)
  blocking collectives  33.2 us (17%)
  between operations  14.4 us (7%)
  local copies, waits for them, and re-layouts  11.2 us (6%)
  other arithmetic  6.44 us (3%)
  matrix products  5.28 us (3%)
  Pallas kernels  4.83 us (2%)
    ppermute x5, starting transfers between devices, swap(): return lax.ppermute(block, axis, [(0, 1), (1, 0)])  47.8 us
    ppermute x5, waiting for transfers between devices, swap(): return lax.ppermute(block, axis, [(0, 1), (1, 0)])  24.3 us
    all_to_all x1, waiting for transfers between devices, local(): got = lax.all_to_all(both, 'l', split_axis=0, concat_axis=0, tiled=True)  22.9 us
    all_to_all x1, blocking collectives, spread_x(): lax.all_to_all(jnp.broadcast_to(block[None], (lax.axis_size('x'), *block....  17.1 us
    all_to_all x1, blocking collectives, local(): part = lax.all_to_all(scaled, 'y', split_axis=0, concat_axis=0, tiled=True)  16.1 us
    all_to_all x3, starting transfers between devices, spread_x(): lax.all_to_all(jnp.broadcast_to(block[None], (lax.axis_size('x'), *block....  12.3 us
    all_to_all x1, waiting for transfers between devices, local(): mine = lax.all_to_all(sent, 'x', split_axis=0, concat_axis=0, tiled=True)  5.34 us
    dot_general x2, matrix products, product(): lax.dot_general(left.reshape(-1, rows), both, (((0,), (0,)), ((), ())), p...  5.28 us
  transfers between devices with their start and end apart: 12, of which 7 were waited for; matrix products, arithmetic and copies ran while one was open for 9% of the time, Pallas kernels for 0%

profile of v1, /device:TPU:1, one launch (start us, length us, event | category | flops | bytes accessed | tf_op | source)
XLA Modules:
  0.0 196.4 jit_solution(12383104832728844462)
XLA Ops:
  7.2 1.2 reshape.61
  8.4 0.6 broadcast_select_fusion.1
  9.0 0.3 copy_bitcast_fusion.1
  9.3 0.7 maximum_bitcast_fusion
  10.0 4.8 %all-to-all-start = ((bf16[4,32,1024]{2,1,0:T(8,128)(2,1)}), bf16[4,32,1024]{2,1,0:T(8,128)(2,1)S(1)}, u32[]{:S(2)}, u32[]{:S(2)}) async-start(bf16[4,32,1024]{2,1,0:T(8,128)(2,1)} %maximum_bitcast_fusion), calls=%async_computation | async-start | bytes 524288 | tf_op jit(solution)/shard_map/all_to_all | solution.py:117
  14.9 0.2 multiply_reduce_fusion
  15.1 5.3 %all-to-all-done = bf16[4,32,1024]{2,1,0:T(8,128)(2,1)S(1)} async-done(((bf16[4,32,1024]{2,1,0:T(8,128)(2,1)}), bf16[4,32,1024]{2,1,0:T(8,128)(2,1)S(1)}, u32[]{:S(2)}, u32[]{:S(2)}) %all-to-all-start) | async-done | bytes 262176 | tf_op jit(solution)/shard_map/all_to_all | solution.py:117
  20.4 10.7 %collective-permute-start = (bf16[4,16,1024]{2,1,0:T(8,128)(2,1)S(1)}, bf16[4,16,1024]{2,1,0:T(8,128)(2,1)S(1)}, u32[]{:S(2)}, u32[]{:S(2)}) collective-permute-start(bf16[4,16,1024]{2,1,0:T(8,128)(2,1)S(1)} %get-tuple-element.30), channel_id=1, source_target_pairs={{0,64},{64,0},{1,65},{65,1},{2,66},{66,2},{3,67},{67,3},{4,68},{68... | collective-permute-start | bytes 393224 | tf_op jit(solution)/shard_map/ppermute | solution.py:32
  31.1 2.4 %collective-permute-done = bf16[4,16,1024]{2,1,0:T(8,128)(2,1)S(1)} collective-permute-done((bf16[4,16,1024]{2,1,0:T(8,128)(2,1)S(1)}, bf16[4,16,1024]{2,1,0:T(8,128)(2,1)S(1)}, u32[]{:S(2)}, u32[]{:S(2)}) %collective-permute-start) | collective-permute-done | bytes 131104 | tf_op jit(solution)/shard_map/ppermute | solution.py:32
  33.5 0.7 pad_maximum_fusion.1
  34.4 0.2 reshape.63
  34.7 0.1 fusion
  34.9 0.2 reshape.64
  35.0 16.1 %all_to_all.35 = bf16[8,16,1024]{2,1,0:T(8,128)(2,1)S(1)} all-to-all(bf16[8,16,1024]{2,1,0:T(8,128)(2,1)S(1)} %reshape.64), channel_id=1, replica_groups=mesh['x'=4,'h'=2,'y'=8,'l'=4,'c'=2] {'y'}, dimensions={0} | all-to-all | bytes 524288 | tf_op jit(solution)/shard_map/all_to_all | solution.py:127
  51.1 1.1 broadcast_in_dim.28
  52.2 3.5 %all-to-all-start.2 = ((bf16[4,8,16,1024]{3,2,1,0:T(8,128)(2,1)}), bf16[4,8,16,1024]{3,2,1,0:T(8,128)(2,1)S(1)}, u32[]{:S(2)}, u32[]{:S(2)}) async-start(bf16[4,8,16,1024]{3,2,1,0:T(8,128)(2,1)} %broadcast_in_dim.28), calls=%async_computation.2 | async-start | bytes 2097152 | tf_op jit(solution)/shard_map/all_to_all | solution.py:26
  55.7 8.2 %collective-permute-start.1 = (bf16[8,16,1024]{2,1,0:T(8,128)(2,1)S(1)}, bf16[8,16,1024]{2,1,0:T(8,128)(2,1)S(1)}, u32[]{:S(2)}, u32[]{:S(2)}) collective-permute-start(bf16[8,16,1024]{2,1,0:T(8,128)(2,1)S(1)} %all_to_all.35), channel_id=1, source_target_pairs={{0,64},{64,0},{1,65},{65,1},{2,66},{66,2},{3,67},{67,3},{4,68},{68... | collective-permute-start | bytes 786440 | tf_op jit(solution)/shard_map/ppermute | solution.py:32
  64.0 3.7 %collective-permute-done.1 = bf16[8,16,1024]{2,1,0:T(8,128)(2,1)S(1)} collective-permute-done((bf16[8,16,1024]{2,1,0:T(8,128)(2,1)S(1)}, bf16[8,16,1024]{2,1,0:T(8,128)(2,1)S(1)}, u32[]{:S(2)}, u32[]{:S(2)}) %collective-permute-start.1) | collective-permute-done | bytes 262176 | tf_op jit(solution)/shard_map/ppermute | solution.py:32
  67.7 1.3 broadcast_in_dim.29
  69.0 4.3 %all-to-all-start.3 = ((bf16[4,8,16,1024]{3,2,1,0:T(8,128)(2,1)}), bf16[4,8,16,1024]{3,2,1,0:T(8,128)(2,1)}, u32[]{:S(2)}, u32[]{:S(2)}) async-start(bf16[4,8,16,1024]{3,2,1,0:T(8,128)(2,1)} %broadcast_in_dim.29), calls=%async_computation.3 | async-start | bytes 2097152 | tf_op jit(solution)/shard_map/all_to_all | solution.py:26
  73.5 10.1 %collective-permute-start.3 = (bf16[8,128,128]{2,1,0:T(8,128)(2,1)S(1)}, bf16[8,128,128]{2,1,0:T(8,128)(2,1)}, u32[]{:S(2)}, u32[]{:S(2)}) collective-permute-start(bf16[8,128,128]{2,1,0:T(8,128)(2,1)S(1)} %bitcast.51), channel_id=1, source_target_pairs={{0,64},{64,0},{1,65},{65,1},{2,66},{66,2},{3,67},{67,3},{4,68},{68... | collective-permute-start | bytes 786440 | tf_op jit(solution)/shard_map/ppermute | solution.py:32
  83.6 0.7 dynamic_slice.6
  84.3 1.3 constant_dynamic-update-slice_fusion.1
  85.6 1.9 collective-permute-done.3
  87.6 1.8 pad_maximum_fusion
  89.4 1.3 constant_dynamic-update-slice_fusion
  90.7 1.1 fusion.6
  91.9 3.0 %multiply_convert_fusion = bf16[1024,512]{0,1:T(8,128)(2,1)S(1)} fusion(bf16[1024,1024]{1,0:T(8,128)(2,1)} %bitcast.53, bf16[1024,512]{1,0:T(8,128)(2,1)S(1)} %bitcast.50, f32[1024]{0:T(1024)S(1)} %dynamic_slice.6), kind=kOutput, calls=%fused_computation.1 | convolution fusion | flops 1074790400 | bytes 4198400 | tf_op jit(solution)/shard_map/dot_general | solution.py:152
  94.9 15.6 %collective-permute-start.2 = (bf16[1024,512]{0,1:T(8,128)(2,1)S(1)}, bf16[1024,512]{0,1:T(8,128)(2,1)S(1)}, u32[]{:S(2)}, u32[]{:S(2)}) collective-permute-start(bf16[1024,512]{0,1:T(8,128)(2,1)S(1)} %multiply_convert_fusion), channel_id=1, source_target_pairs={{0,1},{1,0},{2,3},{3,2},{4,5},{5,4},{6,7},{7,6},{8,9},{9,8},{10,11... | collective-permute-start | bytes 3145736 | tf_op jit(solution)/shard_map/ppermute | solution.py:32
  110.7 2.2 %collective-permute-done.2 = bf16[1024,512]{0,1:T(8,128)(2,1)S(1)} collective-permute-done((bf16[1024,512]{0,1:T(8,128)(2,1)S(1)}, bf16[1024,512]{0,1:T(8,128)(2,1)S(1)}, u32[]{:S(2)}, u32[]{:S(2)}) %collective-permute-start.2) | collective-permute-done | bytes 1048608 | tf_op jit(solution)/shard_map/ppermute | solution.py:32
  112.8 2.3 %add_convert_fusion = bf16[1024,512]{0,1:T(8,128)(2,1)} fusion(bf16[1024,512]{0,1:T(8,128)(2,1)S(1)} %collective-permute-done.2, bf16[1024,1024]{1,0:T(8,128)(2,1)S(1)} %bitcast.54, bf16[1024,512]{1,0:T(8,128)(2,1)S(1)} %bitcast.49, f32[1024]{0:T(1024)S(1)} %dynamic_slice.6), kind=kOutput, calls=%fused_computation | convolution fusion | flops 1075838976 | bytes 5246976 | tf_op jit(solution)/shard_map/dot_general | solution.py:152
  115.1 3.5 %all-to-all-start.4 = ((bf16[4,1024,128]{1,2,0:T(8,128)(2,1)}), bf16[4,1024,128]{1,2,0:T(8,128)(2,1)S(1)}, u32[]{:S(2)}, u32[]{:S(2)}) async-start(bf16[4,1024,128]{1,2,0:T(8,128)(2,1)} %bitcast.13), calls=%async_computation.4 | async-start | bytes 2097152 | tf_op jit(solution)/shard_map/all_to_all | solution.py:159
  118.7 0.7 fusion.5
  119.5 0.7 compare_bitcast_fusion
  120.2 0.2 select_reduce_fusion
  120.4 0.1 select_reduce_fusion.1.source_ref
  120.5 0.7 multiply_add_fusion.place_ref
  121.2 22.9 %all-to-all-done.4 = bf16[4,1024,128]{1,2,0:T(8,128)(2,1)S(1)} async-done(((bf16[4,1024,128]{1,2,0:T(8,128)(2,1)}), bf16[4,1024,128]{1,2,0:T(8,128)(2,1)S(1)}, u32[]{:S(2)}, u32[]{:S(2)}) %all-to-all-start.4) | async-done | bytes 1048608 | tf_op jit(solution)/shard_map/all_to_all | solution.py:159
  144.1 0.2 reduce_sum.40
  144.3 0.2 copy.52
  144.5 1.1 broadcast_in_dim.32
  145.6 4.5 %all-to-all-start.5 = ((bf16[4,1024,128]{2,1,0:T(8,128)(2,1)}), bf16[4,1024,128]{2,1,0:T(8,128)(2,1)S(1)}, u32[]{:S(2)}, u32[]{:S(2)}) async-start(bf16[4,1024,128]{2,1,0:T(8,128)(2,1)} %broadcast_in_dim.32), calls=%async_computation.5 | async-start | bytes 2097152 | tf_op jit(solution)/shard_map/all_to_all | solution.py:26
  150.1 3.2 %collective-permute-start.4 = (bf16[1024,128]{0,1:T(8,128)(2,1)S(1)}, bf16[1024,128]{0,1:T(8,128)(2,1)S(1)}, u32[]{:S(2)}, u32[]{:S(2)}) collective-permute-start(bf16[1024,128]{0,1:T(8,128)(2,1)S(1)} %reduce_sum.40), channel_id=1, source_target_pairs={{0,64},{64,0},{1,65},{65,1},{2,66},{66,2},{3,67},{67,3},{4,68},{68... | collective-permute-start | bytes 786440 | tf_op jit(solution)/shard_map/ppermute | solution.py:32
  153.3 14.0 %collective-permute-done.4 = bf16[1024,128]{0,1:T(8,128)(2,1)S(1)} collective-permute-done((bf16[1024,128]{0,1:T(8,128)(2,1)S(1)}, bf16[1024,128]{0,1:T(8,128)(2,1)S(1)}, u32[]{:S(2)}, u32[]{:S(2)}) %collective-permute-start.4) | collective-permute-done | bytes 262176 | tf_op jit(solution)/shard_map/ppermute | solution.py:32
  167.3 0.2 copy.53
  167.5 0.1 broadcast_in_dim.33
  167.6 17.1 %all_to_all.36.other_ref = bf16[4,1024,128]{2,1,0:T(8,128)(2,1)S(1)} all-to-all(bf16[4,1024,128]{2,1,0:T(8,128)(2,1)S(1)} %broadcast_in_dim.33), channel_id=1, replica_groups=mesh['x'=4,'h'=2,'y'=8,'l'=4,'c'=2] {'x'}, dimensions={0} | all-to-all | bytes 2097152 | tf_op jit(solution)/shard_map/all_to_all | solution.py:26
  184.8 4.8 %finish.1 = (f32[8,16384]{1,0:T(8,128)}, f32[8,16384]{1,0:T(8,128)}, bf16[8192,128]{1,0:T(8,128)(2,1)}) custom-call(s32[1]{0:T(128)} %bitcast.h_ref, s32[8]{0:T(128)S(1)} %select_reduce_fusion.1.source_ref, s32[64]{0:T(128)S(1)} %multiply_add_fusion.place_ref, bf16[4,1024,128]{2,1,0:T(8,128)(2,1)S(1)} %all-to-all-done.5.own_ref, ...), custom_call_target="tpu_custom_call" | custom-call | flops 4000000 | bytes 8000000 | tf_op jit(solution)/shard_map/finish/pallas_call | solution.py:78
  (35 shorter events, 0.8 us)
Async XLA Ops:
  7.2 7.7 %copy-start.5 = (bf16[16,8192]{1,0:T(8,128)(2,1)S(1)}, bf16[16,8192]{1,0:T(8,128)(2,1)}, u32[]{:S(2)}) copy-start(bf16[16,8192]{1,0:T(8,128)(2,1)} %param.6) | copy-start | bytes 786436
  8.4 25.9 %copy-start.6 = (bf16[16,8192]{1,0:T(8,128)(2,1)S(1)}, bf16[16,8192]{1,0:T(8,128)(2,1)}, u32[]{:S(2)}) copy-start(bf16[16,8192]{1,0:T(8,128)(2,1)} %param.7) | copy-start | bytes 786436
  10.0 10.4 %all-to-all-start = ((bf16[4,32,1024]{2,1,0:T(8,128)(2,1)}), bf16[4,32,1024]{2,1,0:T(8,128)(2,1)S(1)}, u32[]{:S(2)}, u32[]{:S(2)}) async-start(bf16[4,32,1024]{2,1,0:T(8,128)(2,1)} %maximum_bitcast_fusion), calls=%async_computation | async-start | bytes 524288 | tf_op jit(solution)/shard_map/all_to_all | solution.py:117
  14.9 77.0 %all-gather.5.cloned.1.call-start = ((), (), s32[]{:S(2)}) async-start(), calls=%async_computation.7 | async-start | bytes 2359296 | tf_op jit(solution)/shard_map/all_gather | solution.py:119
  20.4 13.1 %collective-permute-start = (bf16[4,16,1024]{2,1,0:T(8,128)(2,1)S(1)}, bf16[4,16,1024]{2,1,0:T(8,128)(2,1)S(1)}, u32[]{:S(2)}, u32[]{:S(2)}) collective-permute-start(bf16[4,16,1024]{2,1,0:T(8,128)(2,1)S(1)} %get-tuple-element.30), channel_id=1, source_target_pairs={{0,64},{64,0},{1,65},{65,1},{2,66},{66,2},{3,67},{67,3},{4,68},{68... | collective-permute-start | bytes 393224 | tf_op jit(solution)/shard_map/ppermute | solution.py:32
  52.2 15.5 %all-to-all-start.2 = ((bf16[4,8,16,1024]{3,2,1,0:T(8,128)(2,1)}), bf16[4,8,16,1024]{3,2,1,0:T(8,128)(2,1)S(1)}, u32[]{:S(2)}, u32[]{:S(2)}) async-start(bf16[4,8,16,1024]{3,2,1,0:T(8,128)(2,1)} %broadcast_in_dim.28), calls=%async_computation.2 | async-start | bytes 2097152 | tf_op jit(solution)/shard_map/all_to_all | solution.py:26
  55.7 17.6 %copy-start = (f32[1,1,8,16384]{3,2,1,0:T(8,128)S(1)}, f32[1,1,8,16384]{3,2,1,0:T(8,128)}, u32[]{:S(2)}) copy-start(f32[1,1,8,16384]{3,2,1,0:T(8,128)} %param.9) | copy-start | bytes 1572868
  55.7 17.6 %copy-start.1 = (f32[1,1,8,16384]{3,2,1,0:T(8,128)S(1)}, f32[1,1,8,16384]{3,2,1,0:T(8,128)}, u32[]{:S(2)}) copy-start(f32[1,1,8,16384]{3,2,1,0:T(8,128)} %param.10) | copy-start | bytes 1572868
  55.7 12.0 %collective-permute-start.1 = (bf16[8,16,1024]{2,1,0:T(8,128)(2,1)S(1)}, bf16[8,16,1024]{2,1,0:T(8,128)(2,1)S(1)}, u32[]{:S(2)}, u32[]{:S(2)}) collective-permute-start(bf16[8,16,1024]{2,1,0:T(8,128)(2,1)S(1)} %all_to_all.35), channel_id=1, source_target_pairs={{0,64},{64,0},{1,65},{65,1},{2,66},{66,2},{3,67},{67,3},{4,68},{68... | collective-permute-start | bytes 786440 | tf_op jit(solution)/shard_map/ppermute | solution.py:32
  67.7 5.7 %copy-start.3 = (bf16[4,8,16,1024]{3,2,1,0:T(8,128)(2,1)}, bf16[4,8,16,1024]{3,2,1,0:T(8,128)(2,1)S(1)}, u32[]{:S(2)}) copy-start(bf16[4,8,16,1024]{3,2,1,0:T(8,128)(2,1)S(1)} %all-to-all-done.2) | copy-start | bytes 3145732
  69.0 20.4 %all-to-all-start.3 = ((bf16[4,8,16,1024]{3,2,1,0:T(8,128)(2,1)}), bf16[4,8,16,1024]{3,2,1,0:T(8,128)(2,1)}, u32[]{:S(2)}, u32[]{:S(2)}) async-start(bf16[4,8,16,1024]{3,2,1,0:T(8,128)(2,1)} %broadcast_in_dim.29), calls=%async_computation.3 | async-start | bytes 2097152 | tf_op jit(solution)/shard_map/all_to_all | solution.py:26
  73.3 71.0 %all-gather.7.cloned.1.call-start = ((), (), s32[]{:S(2)}) async-start(), calls=%async_computation.8 | async-start | bytes 2621440 | tf_op jit(solution)/shard_map/all_gather | solution.py:138
  73.5 14.1 %collective-permute-start.3 = (bf16[8,128,128]{2,1,0:T(8,128)(2,1)S(1)}, bf16[8,128,128]{2,1,0:T(8,128)(2,1)}, u32[]{:S(2)}, u32[]{:S(2)}) collective-permute-start(bf16[8,128,128]{2,1,0:T(8,128)(2,1)S(1)} %bitcast.51), channel_id=1, source_target_pairs={{0,64},{64,0},{1,65},{65,1},{2,66},{66,2},{3,67},{67,3},{4,68},{68... | collective-permute-start | bytes 786440 | tf_op jit(solution)/shard_map/ppermute | solution.py:32
  91.9 18.6 %copy-start.4 = (bf16[8,8,16,512]{3,2,1,0:T(8,128)(2,1)S(1)}, bf16[8,8,16,512]{3,2,1,0:T(8,128)(2,1)}, u32[]{:S(2)}) copy-start(bf16[8,8,16,512]{3,2,1,0:T(8,128)(2,1)} %get-tuple-element.27) | copy-start | bytes 3145732
  94.9 17.9 %copy-start.7 = (bf16[16,4,16,1024]{3,2,1,0:T(8,128)(2,1)S(1)}, bf16[16,4,16,1024]{3,2,1,0:T(8,128)(2,1)}, u32[]{:S(2)}) copy-start(bf16[16,4,16,1024]{3,2,1,0:T(8,128)(2,1)} %all-gather.5.cloned.1.call-done) | copy-start | bytes 6291460
  94.9 17.9 %collective-permute-start.2 = (bf16[1024,512]{0,1:T(8,128)(2,1)S(1)}, bf16[1024,512]{0,1:T(8,128)(2,1)S(1)}, u32[]{:S(2)}, u32[]{:S(2)}) collective-permute-start(bf16[1024,512]{0,1:T(8,128)(2,1)S(1)} %multiply_convert_fusion), channel_id=1, source_target_pairs={{0,1},{1,0},{2,3},{3,2},{4,5},{5,4},{6,7},{7,6},{8,9},{9,8},{10,11... | collective-permute-start | bytes 3145736 | tf_op jit(solution)/shard_map/ppermute | solution.py:32
  115.1 29.0 %all-to-all-start.4 = ((bf16[4,1024,128]{1,2,0:T(8,128)(2,1)}), bf16[4,1024,128]{1,2,0:T(8,128)(2,1)S(1)}, u32[]{:S(2)}, u32[]{:S(2)}) async-start(bf16[4,1024,128]{1,2,0:T(8,128)(2,1)} %bitcast.13), calls=%async_computation.4 | async-start | bytes 2097152 | tf_op jit(solution)/shard_map/all_to_all | solution.py:159
  145.6 21.7 %all-to-all-start.5 = ((bf16[4,1024,128]{2,1,0:T(8,128)(2,1)}), bf16[4,1024,128]{2,1,0:T(8,128)(2,1)S(1)}, u32[]{:S(2)}, u32[]{:S(2)}) async-start(bf16[4,1024,128]{2,1,0:T(8,128)(2,1)} %broadcast_in_dim.32), calls=%async_computation.5 | async-start | bytes 2097152 | tf_op jit(solution)/shard_map/all_to_all | solution.py:26
  150.1 17.2 %collective-permute-start.4 = (bf16[1024,128]{0,1:T(8,128)(2,1)S(1)}, bf16[1024,128]{0,1:T(8,128)(2,1)S(1)}, u32[]{:S(2)}, u32[]{:S(2)}) collective-permute-start(bf16[1024,128]{0,1:T(8,128)(2,1)S(1)} %reduce_sum.40), channel_id=1, source_target_pairs={{0,64},{64,0},{1,65},{65,1},{2,66},{66,2},{3,67},{67,3},{4,68},{68... | collective-permute-start | bytes 786440 | tf_op jit(solution)/shard_map/ppermute | solution.py:32
  167.5 17.3 %copy-start.2 = (bf16[8,8,128,128]{3,2,1,0:T(8,128)(2,1)S(1)}, bf16[8,8,128,128]{3,2,1,0:T(8,128)(2,1)}, u32[]{:S(2)}) copy-start(bf16[8,8,128,128]{3,2,1,0:T(8,128)(2,1)} %all-gather.7.cloned.1.call-done) | copy-start | bytes 6291460
Sparse Core Ops, SparseCore 0:
  34.4 43.5 all-gather.4
  89.5 44.2 all-gather.6

commit v2 on v1

v2 whole, which is shorter than its diff:
```python
import functools

import jax
import jax.numpy as jnp
from jax import lax
from jax.experimental import pallas as pl
from jax.experimental.pallas import tpu as pltpu
from jax.sharding import Mesh, PartitionSpec as P

norm_eps = 1e-05
momentum_rate = 0.9
learn_rate = 0.2

PARTS = (("x", 4), ("h", 2), ("y", 8), ("l", 4), ("c", 2))
GROUP = ("x", "h")
DEV = ("y", "l", "c")


def slot_table(owner_row, groups):
    onehot = (owner_row[:, None] == jnp.arange(groups, dtype=jnp.int32)[None, :]).astype(jnp.int32)
    before = jnp.cumsum(onehot, axis=0) - onehot
    return jnp.sum(before * onehot, axis=1)


def spread(block, axis):
    return lax.all_to_all(
        jnp.broadcast_to(block[None], (lax.axis_size(axis), *block.shape)), axis, split_axis=0, concat_axis=0, tiled=True
    )


def swap(block, axis):
    return lax.ppermute(block, axis, [(0, 1), (1, 0)])


def finish_kernel(per_group, part_rows, h_ref, source_ref, place_ref, own_ref, other_ref, pulled_ref, base_master_ref,
                  base_momentum_ref, master_out, momentum_out, params_out, work_ref):
    x = pl.program_id(0)
    h = h_ref[0]
    columns = params_out.shape[1]
    span = per_group * part_rows
    for theirs in range(2):
        block = lax.rem(h + theirs, 2)
        grad_ref = (own_ref, other_ref)[theirs]
        for p in range(per_group):
            held = pulled_ref[place_ref[(x * 2 + block) * per_group + p]].astype(jnp.float32)
            grad = grad_ref[x, p * part_rows : (p + 1) * part_rows, :].astype(jnp.float32)
            rows = pl.ds(pl.multiple_of(block * span + p * part_rows, part_rows), part_rows)
            params_out[rows, :] = (held - learn_rate * grad).astype(jnp.bfloat16)

    step = base_master_ref.shape[1] // columns
    for j in range(per_group):
        k = source_ref[j]
        block = lax.div(k, per_group)
        start = pl.multiple_of(lax.rem(k, per_group) * part_rows + x * step, step)
        bx = lax.div(block, 2)
        mine = own_ref[bx, pl.ds(start, step), :].astype(jnp.float32)
        theirs = other_ref[bx, pl.ds(start, step), :].astype(jnp.float32)
        work_ref[pl.ds(j * step, step), :] = jnp.where(lax.rem(block, 2) == h, mine, theirs)
    for r in range(step):
        grad = work_ref[pl.ds(r, per_group, stride=step), :]
        cols = pl.ds(r * columns, columns)
        momentum_out[:, cols] = base_momentum_ref[:, cols] + grad
        master_out[:, cols] = base_master_ref[:, cols] - learn_rate * grad


def finish(h, source, place, own, other, pulled, master, momentum):
    nx, rows, columns = own.shape
    part_count, part_rows, _ = pulled.shape
    per_group, part_size = master.shape
    groups = part_count // per_group
    whole = lambda arr: pl.BlockSpec(arr.shape, lambda a, *_: (0,) * arr.ndim)
    served = pl.BlockSpec((per_group, part_size // nx), lambda a, *_: (0, a))
    return pl.pallas_call(
        functools.partial(finish_kernel, per_group, part_rows),
        grid_spec=pltpu.PrefetchScalarGridSpec(
            num_scalar_prefetch=3,
            grid=(nx,),
            in_specs=[whole(own), whole(other), whole(pulled), served, served],
            out_specs=[served, served, pl.BlockSpec((groups // nx * rows, columns), lambda a, *_: (a, 0))],
            scratch_shapes=[pltpu.VMEM((per_group * part_rows // nx, columns), jnp.float32)],
        ),
        out_shape=[
            jax.ShapeDtypeStruct(master.shape, jnp.float32),
            jax.ShapeDtypeStruct(master.shape, jnp.float32),
            jax.ShapeDtypeStruct((groups * rows, columns), jnp.bfloat16),
        ],
        compiler_params=pltpu.CompilerParams(vmem_limit_bytes=24 * 1024 * 1024),
        cost_estimate=pl.CostEstimate(flops=4_000_000, bytes_accessed=8_000_000, transcendentals=0),
        name="finish",
    )(h.reshape(1), source, place, own, other, pulled, master, momentum)


def local(tokens, query_grad, gain, master, momentum, owner):
    nx, nh, ny, nl, nc = (lax.axis_size(name) for name, _ in PARTS)
    groups = nx * nh
    own, width = tokens.shape
    columns = width // (ny * nl * nc)
    rows = width // groups
    part_size = master.shape[-1]
    part_count = owner.shape[1]
    per_group = part_count // groups
    part_rows = part_size // columns
    h = lax.axis_index("h")
    c = lax.axis_index("c")
    me = lax.axis_index(GROUP)

    sent = tokens.reshape(own, nx, nc, rows)
    sent = jnp.concatenate(
        [jnp.where(c == 0, sent[:, :, 0], sent[:, :, 1]), jnp.where(c == 0, sent[:, :, 1], sent[:, :, 0])], axis=0
    )
    sent = sent.transpose(1, 0, 2)
    mine = lax.all_to_all(sent, "x", split_axis=0, concat_axis=0, tiled=True)
    pair = jnp.stack([mine[:, :own], swap(mine[:, own:], "c")])
    left = lax.all_gather(pair, "y", axis=0, tiled=False)

    values = tokens.astype(jnp.float32)
    scale = lax.rsqrt(jnp.mean(values * values, axis=1, keepdims=True) + norm_eps)
    scaled = (query_grad.astype(jnp.float32) * scale).astype(jnp.bfloat16)
    scaled = scaled.reshape(own, ny, nl, nc, columns)
    scaled = jnp.where(c == 0, scaled, scaled[:, :, :, ::-1])
    scaled = scaled.transpose(1, 0, 3, 2, 4).reshape(ny, own, nc * nl * columns)

    def past(master, momentum):
        block = (master - learn_rate * momentum_rate * momentum).astype(jnp.bfloat16)
        return block.reshape(per_group, part_rows, columns)

    scaled, pair = lax.optimization_barrier((scaled, pair))
    part = lax.all_to_all(scaled, "y", split_axis=0, concat_axis=0, tiled=True)
    before_other, part = lax.optimization_barrier((past(master[0, 0], momentum[0, 0]), part))
    before_other = swap(before_other, "h")
    right_own = spread(part, "x")
    right_own, before_other = lax.optimization_barrier((right_own, before_other))
    right_other = swap(right_own, "c")
    half = nl * columns
    halves = [
        jnp.concatenate([right_own[..., :half], right_other[..., half:]]),
        jnp.concatenate([right_own[..., half:], right_other[..., :half]]),
    ]

    owner_row = lax.dynamic_slice_in_dim(owner, lax.axis_index(DEV), 1, 0)[0]
    rank = slot_table(owner_row, groups)
    place = (jnp.where(owner_row % nh == h, 0, nx) + owner_row // nh) * per_group + rank
    slots = jnp.arange(per_group, dtype=jnp.int32)
    hit = (owner_row[None, :] == me) & (rank[None, :] == slots[:, None])
    source = jnp.sum(jnp.where(hit, jnp.arange(part_count, dtype=jnp.int32)[None, :], 0), axis=1)

    weight = lax.dynamic_slice_in_dim(gain, (lax.axis_index("x") * nc + c) * rows, rows, 0)[:, None]

    def product(right):
        out = lax.dot_general(
            left.reshape(-1, rows),
            right.transpose(1, 0, 2, 3).reshape(-1, half),
            (((0,), (0,)), ((), ())),
            preferred_element_type=jnp.float32,
        )
        return (weight * out).astype(jnp.bfloat16)

    came = swap(product(halves[1]), "c")
    keep = product(halves[0])
    both = jnp.concatenate([block.reshape(rows, nl, columns).transpose(1, 0, 2) for block in (keep, came)])
    both = both.reshape(nh * nl * rows, columns)
    summed = lax.psum_scatter(both, ("h", "l"), scatter_dimension=0, tiled=True)

    base_master, base_momentum, _ = lax.optimization_barrier((master[0, 0], momentum[0, 0], came))
    before_own = spread(past(base_master, base_momentum), "x")
    before_own, before_other = lax.optimization_barrier((before_own, before_other))
    before_other = spread(before_other, "x")
    pulled = jnp.concatenate([before_own, before_other]).reshape(part_count, part_rows, columns)
    base_master = base_master - learn_rate * momentum_rate * base_momentum
    base_momentum = momentum_rate * base_momentum
    summed, pulled, place, source, base_master, base_momentum = lax.optimization_barrier(
        (summed, pulled, place, source, base_master, base_momentum)
    )

    full_own = lax.all_gather(summed, "x", axis=0, tiled=False)
    full_other = spread(swap(summed, "h"), "x")
    master_new, momentum_new, params_new = finish(
        lax.rem(h + c, nh), source, place, full_own, full_other, pulled, base_master, base_momentum
    )
    return (master_new[None, None], momentum_new[None, None], params_new)


def solution(mesh):
    fine = Mesh(mesh.devices.reshape([size for _, size in PARTS]), [name for name, _ in PARTS])
    whole = (*GROUP, *DEV)
    server = P(DEV, GROUP, None, None)
    return jax.shard_map(
        local,
        mesh=fine,
        in_specs=(P(whole, None), P(whole, None), P(), server, server, P()),
        out_specs=(server, server, P(None, DEV)),
        check_vma=False,
    )
```

time: 199 us -> 186 us (0.935)
  blocking collectives: 33.2 us -> 0 us
  waiting for transfers between devices: 52.5 us -> 79.6 us
  starting transfers between devices: 68.5 us -> 59.4 us
  local copies, waits for them, and re-layouts: 11.2 us -> 16.9 us
    all_to_all x4 -> x5, waiting for transfers between devices: 22.9 us -> 61.8 us  [the longest x4 49.7 us: spread(): lax.all_to_all(jnp.broadcast_to(block[None], (lax.axis_size(axis), *block...]
    all_to_all x2 -> x0, blocking collectives: 33.2 us -> none  [the longest x1 17.1 us: spread_x(): lax.all_to_all(jnp.broadcast_to(block[None], (lax.axis_size('x'), *block....]
    ppermute x5, starting transfers between devices: 47.8 us -> 30.8 us  [swap(): return lax.ppermute(block, axis, [(0, 1), (1, 0)])]
    ppermute x5, waiting for transfers between devices: 24.3 us -> 12.3 us  [swap(): return lax.ppermute(block, axis, [(0, 1), (1, 0)])]
    all_to_all x4 -> x5, starting transfers between devices: 15.8 us -> 23.6 us  [the longest x4 20.2 us: spread(): lax.all_to_all(jnp.broadcast_to(block[None], (lax.axis_size(axis), *block...]
    broadcast_in_dim x4 -> x5, local copies, waits for them, and re-layouts: 3.65 us -> 4.71 us  [spread(): jnp.broadcast_to(block[None], (lax.axis_size(axis), *block.shape))]
  transfers between devices with their start and end apart: 12 -> 14, of which waited for: 7 -> 11; matrix products, arithmetic and copies ran while one was open for 9% -> 9% of each run, Pallas kernels for 0% -> 0%
where the time goes in v2:
time: 186 us; the launch traced here: 185 us
  waiting for transfers between devices  79.6 us (43%)
  starting transfers between devices  59.4 us (32%)
  local copies, waits for them, and re-layouts  16.9 us (9%)
  between operations  14.1 us (8%)
  other arithmetic  7.31 us (4%)
  matrix products  4.2 us (2%)
  Pallas kernels  3.12 us (2%)
    all_to_all x4, waiting for transfers between devices, spread(): lax.all_to_all(jnp.broadcast_to(block[None], (lax.axis_size(axis), *block...  49.7 us
    ppermute x5, starting transfers between devices, swap(): return lax.ppermute(block, axis, [(0, 1), (1, 0)])  30.8 us
    all_to_all x4, starting transfers between devices, spread(): lax.all_to_all(jnp.broadcast_to(block[None], (lax.axis_size(axis), *block...  20.2 us
    ppermute x5, waiting for transfers between devices, swap(): return lax.ppermute(block, axis, [(0, 1), (1, 0)])  12.3 us
    all_to_all x1, waiting for transfers between devices, local(): part = lax.all_to_all(scaled, 'y', split_axis=0, concat_axis=0, tiled=True)  12.2 us
    all_to_all x1, waiting for transfers between devices, local(): mine = lax.all_to_all(sent, 'x', split_axis=0, concat_axis=0, tiled=True)  5.34 us
    all_to_all x1, starting transfers between devices, local(): mine = lax.all_to_all(sent, 'x', split_axis=0, concat_axis=0, tiled=True)  4.84 us
    broadcast_in_dim x5, local copies, waits for them, and re-layouts, spread(): jnp.broadcast_to(block[None], (lax.axis_size(axis), *block.shape))  4.71 us
  transfers between devices with their start and end apart: 14, of which 11 were waited for; matrix products, arithmetic and copies ran while one was open for 9% of the time, Pallas kernels for 0%

profile of v2, /device:TPU:1, one launch (start us, length us, event | category | flops | bytes accessed | tf_op | source)
XLA Modules:
  0.0 184.5 jit_solution(1237095120389932805)
XLA Ops:
  7.2 1.2 reshape.67
  8.4 0.6 broadcast_select_fusion.1
  9.0 0.3 copy_bitcast_fusion
  9.3 0.7 maximum_bitcast_fusion
  10.0 4.8 %all-to-all-start = ((bf16[4,32,1024]{2,1,0:T(8,128)(2,1)}), bf16[4,32,1024]{2,1,0:T(8,128)(2,1)S(1)}, u32[]{:S(2)}, u32[]{:S(2)}) async-start(bf16[4,32,1024]{2,1,0:T(8,128)(2,1)} %maximum_bitcast_fusion), calls=%async_computation | async-start | bytes 524288 | tf_op jit(solution)/shard_map/all_to_all | solution.py:112
  14.9 0.2 multiply_reduce_fusion
  15.1 5.3 %all-to-all-done = bf16[4,32,1024]{2,1,0:T(8,128)(2,1)S(1)} async-done(((bf16[4,32,1024]{2,1,0:T(8,128)(2,1)}), bf16[4,32,1024]{2,1,0:T(8,128)(2,1)S(1)}, u32[]{:S(2)}, u32[]{:S(2)}) %all-to-all-start) | async-done | bytes 262176 | tf_op jit(solution)/shard_map/all_to_all | solution.py:112
  20.5 8.6 %collective-permute-start = (bf16[4,16,1024]{2,1,0:T(8,128)(2,1)S(1)}, bf16[4,16,1024]{2,1,0:T(8,128)(2,1)S(1)}, u32[]{:S(2)}, u32[]{:S(2)}) collective-permute-start(bf16[4,16,1024]{2,1,0:T(8,128)(2,1)S(1)} %get-tuple-element.47), channel_id=1, source_target_pairs={{0,1},{1,0},{2,3},{3,2},{4,5},{5,4},{6,7},{7,6},{8,9},{9,8},{10,11... | collective-permute-start | bytes 393224 | tf_op jit(solution)/shard_map/ppermute | solution.py:32
  29.1 1.0 collective-permute-done
  30.0 0.7 pad_maximum_fusion.4
  31.3 0.9 reshape.70
  32.2 3.4 %all-to-all-start.1 = ((bf16[8,16,1024]{2,1,0:T(8,128)(2,1)}), bf16[8,16,1024]{2,1,0:T(8,128)(2,1)S(1)}, u32[]{:S(2)}, u32[]{:S(2)}) async-start(bf16[8,16,1024]{2,1,0:T(8,128)(2,1)} %reshape.70), calls=%async_computation.1 | async-start | bytes 524288 | tf_op jit(solution)/shard_map/all_to_all | solution.py:128
  35.7 12.2 %all-to-all-done.1 = bf16[8,16,1024]{2,1,0:T(8,128)(2,1)S(1)} async-done(((bf16[8,16,1024]{2,1,0:T(8,128)(2,1)}), bf16[8,16,1024]{2,1,0:T(8,128)(2,1)S(1)}, u32[]{:S(2)}, u32[]{:S(2)}) %all-to-all-start.1) | async-done | bytes 262176 | tf_op jit(solution)/shard_map/all_to_all | solution.py:128
  47.9 1.1 broadcast_in_dim.32
  49.0 3.5 %all-to-all-start.2 = ((bf16[4,8,16,1024]{3,2,1,0:T(8,128)(2,1)}), bf16[4,8,16,1024]{3,2,1,0:T(8,128)(2,1)S(1)}, u32[]{:S(2)}, u32[]{:S(2)}) async-start(bf16[4,8,16,1024]{3,2,1,0:T(8,128)(2,1)} %broadcast_in_dim.32), calls=%async_computation.2 | async-start | bytes 2097152 | tf_op jit(solution)/shard_map/all_to_all | solution.py:26
  52.6 8.5 %collective-permute-start.1 = (bf16[8,128,128]{2,0,1:T(8,128)(2,1)S(1)}, bf16[8,128,128]{2,0,1:T(8,128)(2,1)S(1)}, u32[]{:S(2)}, u32[]{:S(2)}) collective-permute-start(bf16[8,128,128]{2,0,1:T(8,128)(2,1)S(1)} %fusion.1), channel_id=1, source_target_pairs={{0,64},{64,0},{1,65},{65,1},{2,66},{66,2},{3,67},{67,3},{4,68},{68... | collective-permute-start | bytes 786440 | tf_op jit(solution)/shard_map/ppermute | solution.py:32
  61.0 4.3 %collective-permute-done.1 = bf16[8,128,128]{2,0,1:T(8,128)(2,1)S(1)} collective-permute-done((bf16[8,128,128]{2,0,1:T(8,128)(2,1)S(1)}, bf16[8,128,128]{2,0,1:T(8,128)(2,1)S(1)}, u32[]{:S(2)}, u32[]{:S(2)}) %collective-permute-start.1) | collective-permute-done | bytes 262176 | tf_op jit(solution)/shard_map/ppermute | solution.py:32
  65.4 1.7 all-to-all-done.2
  67.1 1.0 copy.55
  68.1 3.4 %collective-permute-start.2 = (bf16[4,8,16,1024]{3,2,0,1:T(8,128)(2,1)}, bf16[4,8,16,1024]{3,2,0,1:T(8,128)(2,1)}, u32[]{:S(2)}, u32[]{:S(2)}) collective-permute-start(bf16[4,8,16,1024]{3,2,0,1:T(8,128)(2,1)} %copy.55), channel_id=1, source_target_pairs={{0,1},{1,0},{2,3},{3,2},{4,5},{5,4},{6,7},{7,6},{8,9},{9,8},{10,11... | collective-permute-start | bytes 3145736 | tf_op jit(solution)/shard_map/ppermute | solution.py:32
  71.5 0.7 dynamic_slice.6
  72.3 1.8 collective-permute-done.2
  74.1 1.3 fusion.7
  75.5 2.9 %multiply_convert_fusion = bf16[1024,512]{0,1:T(8,128)(2,1)S(1)} fusion(bf16[1024,1024]{1,0:T(8,128)(2,1)} %bitcast.56, bf16[1024,512]{1,0:T(8,128)(2,1)S(1)} %bitcast.51, f32[1024]{0:T(1024)S(1)} %dynamic_slice.6), kind=kOutput, calls=%fused_computation.2 | convolution fusion | flops 1074790400 | bytes 4198400 | tf_op jit(solution)/shard_map/dot_general | solution.py:150
  78.4 2.4 %collective-permute-start.3 = (bf16[1024,512]{0,1:T(8,128)(2,1)S(1)}, bf16[1024,512]{0,1:T(8,128)(2,1)S(1)}, u32[]{:S(2)}, u32[]{:S(2)}) collective-permute-start(bf16[1024,512]{0,1:T(8,128)(2,1)S(1)} %multiply_convert_fusion), channel_id=1, source_target_pairs={{0,1},{1,0},{2,3},{3,2},{4,5},{5,4},{6,7},{7,6},{8,9},{9,8},{10,11... | collective-permute-start | bytes 3145736 | tf_op jit(solution)/shard_map/ppermute | solution.py:32
  80.9 1.3 multiply_convert_fusion.1
  82.3 0.8 collective-permute-done.3
  83.3 2.4 %copy.59 = bf16[8,1024,128]{2,1,0:T(8,128)(2,1)} copy(bf16[8,1024,128]{1,2,0:T(8,128)(2,1)S(1)} %pad_maximum_fusion) | data formatting | bytes 4194304 | tf_op jit(solution)/shard_map/concatenate | solution.py:160
  85.7 1.1 convert_bitcast_fusion
  86.8 1.3 broadcast_in_dim.34
  88.1 8.9 %all-to-all-start.3 = ((bf16[4,8,128,128]{3,2,1,0:T(8,128)(2,1)}), bf16[4,8,128,128]{3,2,1,0:T(8,128)(2,1)S(1)}, u32[]{:S(2)}, u32[]{:S(2)}) async-start(bf16[4,8,128,128]{3,2,1,0:T(8,128)(2,1)} %broadcast_in_dim.34), calls=%async_computation.4 | async-start | bytes 2097152 | tf_op jit(solution)/shard_map/all_to_all | solution.py:26
  97.0 0.7 fusion.5
  97.6 13.8 %all-to-all-done.3 = bf16[4,8,128,128]{3,2,1,0:T(8,128)(2,1)S(1)} async-done(((bf16[4,8,128,128]{3,2,1,0:T(8,128)(2,1)}), bf16[4,8,128,128]{3,2,1,0:T(8,128)(2,1)S(1)}, u32[]{:S(2)}, u32[]{:S(2)}) %all-to-all-start.3) | async-done | bytes 1048608 | tf_op jit(solution)/shard_map/all_to_all | solution.py:26
  111.5 1.2 broadcast_in_dim.58
  112.7 4.2 %all-to-all-start.4 = ((bf16[4,8,128,128]{3,2,1,0:T(8,128)(2,1)}), bf16[4,8,128,128]{3,2,1,0:T(8,128)(2,1)}, u32[]{:S(2)}, u32[]{:S(2)}) async-start(bf16[4,8,128,128]{3,2,1,0:T(8,128)(2,1)} %broadcast_in_dim.58), calls=%async_computation.5 | async-start | bytes 2097152 | tf_op jit(solution)/shard_map/all_to_all | solution.py:26
  117.2 0.7 compare_bitcast_fusion
  118.2 0.7 multiply_add_fusion.place_ref
  118.9 11.7 %all-to-all-done.4 = bf16[4,8,128,128]{3,2,1,0:T(8,128)(2,1)} async-done(((bf16[4,8,128,128]{3,2,1,0:T(8,128)(2,1)}), bf16[4,8,128,128]{3,2,1,0:T(8,128)(2,1)}, u32[]{:S(2)}, u32[]{:S(2)}) %all-to-all-start.4) | async-done | bytes 1048608 | tf_op jit(solution)/shard_map/all_to_all | solution.py:26
  130.7 1.4 pad_maximum_fusion.1
  132.1 8.0 %collective-permute-start.4 = (bf16[1024,128]{1,0:T(8,128)(2,1)}, bf16[1024,128]{1,0:T(8,128)(2,1)S(1)}, u32[]{:S(2)}, u32[]{:S(2)}) collective-permute-start(bf16[1024,128]{1,0:T(8,128)(2,1)} %reduce-scatter.2.cloned.1.call-done), channel_id=1, source_target_pairs={{0,64},{64,0},{1,65},{65,1},{2,66},{66,2},{3,67},{67,3},{4,68},{68... | collective-permute-start | bytes 786440 | tf_op jit(solution)/shard_map/ppermute | solution.py:32
  140.1 4.4 %collective-permute-done.4 = bf16[1024,128]{1,0:T(8,128)(2,1)S(1)} collective-permute-done((bf16[1024,128]{1,0:T(8,128)(2,1)}, bf16[1024,128]{1,0:T(8,128)(2,1)S(1)}, u32[]{:S(2)}, u32[]{:S(2)}) %collective-permute-start.4) | collective-permute-done | bytes 262176 | tf_op jit(solution)/shard_map/ppermute | solution.py:32
  144.5 1.1 broadcast_in_dim.62
  145.6 3.5 %all-to-all-start.5 = ((bf16[4,1024,128]{2,1,0:T(8,128)(2,1)}), bf16[4,1024,128]{2,1,0:T(8,128)(2,1)S(1)}, u32[]{:S(2)}, u32[]{:S(2)}) async-start(bf16[4,1024,128]{2,1,0:T(8,128)(2,1)} %broadcast_in_dim.62), calls=%async_computation.6 | async-start | bytes 2097152 | tf_op jit(solution)/shard_map/all_to_all | solution.py:26
  149.1 22.4 %all-to-all-done.5.other_ref = bf16[4,1024,128]{2,1,0:T(8,128)(2,1)S(1)} async-done(((bf16[4,1024,128]{2,1,0:T(8,128)(2,1)}), bf16[4,1024,128]{2,1,0:T(8,128)(2,1)S(1)}, u32[]{:S(2)}, u32[]{:S(2)}) %all-to-all-start.5) | async-done | bytes 1048608 | tf_op jit(solution)/shard_map/all_to_all | solution.py:26
  171.5 1.0 copy-done
  172.6 1.0 copy-done.1
  173.6 1.2 copy-done.2
  174.9 3.1 %finish.1 = (f32[8,16384]{1,0:T(8,128)}, f32[8,16384]{1,0:T(8,128)}, bf16[8192,128]{1,0:T(8,128)(2,1)}) custom-call(s32[1]{0:T(128)} %bitcast.h_ref, s32[8]{0:T(128)S(1)} %select_reduce_fusion.1.source_ref, s32[64]{0:T(128)S(1)} %multiply_add_fusion.place_ref, bf16[4,1024,128]{2,1,0:T(8,128)(2,1)S(1)} %bitcast.47, ...), custom_call_target="tpu_custom_call" | custom-call | flops 4000000 | bytes 8000000 | tf_op jit(solution)/shard_map/finish/pallas_call | solution.py:73
  (39 shorter events, 1.8 us)
Async XLA Ops:
  7.2 7.7 %copy-start.5 = (bf16[16,8192]{1,0:T(8,128)(2,1)S(1)}, bf16[16,8192]{1,0:T(8,128)(2,1)}, u32[]{:S(2)}) copy-start(bf16[16,8192]{1,0:T(8,128)(2,1)} %param.6) | copy-start | bytes 786436
  8.4 22.4 %copy-start.6 = (bf16[16,8192]{1,0:T(8,128)(2,1)S(1)}, bf16[16,8192]{1,0:T(8,128)(2,1)}, u32[]{:S(2)}) copy-start(bf16[16,8192]{1,0:T(8,128)(2,1)} %param.7) | copy-start | bytes 786436
  10.0 10.4 %all-to-all-start = ((bf16[4,32,1024]{2,1,0:T(8,128)(2,1)}), bf16[4,32,1024]{2,1,0:T(8,128)(2,1)S(1)}, u32[]{:S(2)}, u32[]{:S(2)}) async-start(bf16[4,32,1024]{2,1,0:T(8,128)(2,1)} %maximum_bitcast_fusion), calls=%async_computation | async-start | bytes 524288 | tf_op jit(solution)/shard_map/all_to_all | solution.py:112
  14.9 60.6 %all-gather.5.cloned.1.call-start = ((), (), s32[]{:S(2)}) async-start(), calls=%async_computation.8 | async-start | bytes 2359296 | tf_op jit(solution)/shard_map/all_gather | solution.py:114
  20.4 15.2 %copy-start.3 = (f32[1,1,8,16384]{3,2,1,0:T(8,128)S(1)}, f32[1,1,8,16384]{3,2,1,0:T(8,128)}, u32[]{:S(2)}) copy-start(f32[1,1,8,16384]{3,2,1,0:T(8,128)} %param.9) | copy-start | bytes 1572868
  20.4 15.2 %copy-start.4 = (f32[1,1,8,16384]{3,2,1,0:T(8,128)S(1)}, f32[1,1,8,16384]{3,2,1,0:T(8,128)}, u32[]{:S(2)}) copy-start(f32[1,1,8,16384]{3,2,1,0:T(8,128)} %param.10) | copy-start | bytes 1572868
  20.5 9.6 %collective-permute-start = (bf16[4,16,1024]{2,1,0:T(8,128)(2,1)S(1)}, bf16[4,16,1024]{2,1,0:T(8,128)(2,1)S(1)}, u32[]{:S(2)}, u32[]{:S(2)}) collective-permute-start(bf16[4,16,1024]{2,1,0:T(8,128)(2,1)S(1)} %get-tuple-element.47), channel_id=1, source_target_pairs={{0,1},{1,0},{2,3},{3,2},{4,5},{5,4},{6,7},{7,6},{8,9},{9,8},{10,11... | collective-permute-start | bytes 393224 | tf_op jit(solution)/shard_map/ppermute | solution.py:32
  32.2 15.7 %all-to-all-start.1 = ((bf16[8,16,1024]{2,1,0:T(8,128)(2,1)}), bf16[8,16,1024]{2,1,0:T(8,128)(2,1)S(1)}, u32[]{:S(2)}, u32[]{:S(2)}) async-start(bf16[8,16,1024]{2,1,0:T(8,128)(2,1)} %reshape.70), calls=%async_computation.1 | async-start | bytes 524288 | tf_op jit(solution)/shard_map/all_to_all | solution.py:128
  49.0 18.1 %all-to-all-start.2 = ((bf16[4,8,16,1024]{3,2,1,0:T(8,128)(2,1)}), bf16[4,8,16,1024]{3,2,1,0:T(8,128)(2,1)S(1)}, u32[]{:S(2)}, u32[]{:S(2)}) async-start(bf16[4,8,16,1024]{3,2,1,0:T(8,128)(2,1)} %broadcast_in_dim.32), calls=%async_computation.2 | async-start | bytes 2097152 | tf_op jit(solution)/shard_map/all_to_all | solution.py:26
  52.5 79.6 %reduce-scatter.2.cloned.1.call-start = ((), (), s32[]{:S(2)}) async-start(), calls=%async_computation.7 | async-start | bytes 2359296 | tf_op jit(solution)/shard_map/reduce_scatter | solution.py:162
  52.6 12.8 %collective-permute-start.1 = (bf16[8,128,128]{2,0,1:T(8,128)(2,1)S(1)}, bf16[8,128,128]{2,0,1:T(8,128)(2,1)S(1)}, u32[]{:S(2)}, u32[]{:S(2)}) collective-permute-start(bf16[8,128,128]{2,0,1:T(8,128)(2,1)S(1)} %fusion.1), channel_id=1, source_target_pairs={{0,64},{64,0},{1,65},{65,1},{2,66},{66,2},{3,67},{67,3},{4,68},{68... | collective-permute-start | bytes 786440 | tf_op jit(solution)/shard_map/ppermute | solution.py:32
  68.1 6.0 %collective-permute-start.2 = (bf16[4,8,16,1024]{3,2,0,1:T(8,128)(2,1)}, bf16[4,8,16,1024]{3,2,0,1:T(8,128)(2,1)}, u32[]{:S(2)}, u32[]{:S(2)}) collective-permute-start(bf16[4,8,16,1024]{3,2,0,1:T(8,128)(2,1)} %copy.55), channel_id=1, source_target_pairs={{0,1},{1,0},{2,3},{3,2},{4,5},{5,4},{6,7},{7,6},{8,9},{9,8},{10,11... | collective-permute-start | bytes 3145736 | tf_op jit(solution)/shard_map/ppermute | solution.py:32
  78.4 2.5 %copy-start.7 = (bf16[16,4,16,1024]{3,2,1,0:T(8,128)(2,1)S(1)}, bf16[16,4,16,1024]{3,2,1,0:T(8,128)(2,1)}, u32[]{:S(2)}) copy-start(bf16[16,4,16,1024]{3,2,1,0:T(8,128)(2,1)} %all-gather.5.cloned.1.call-done) | copy-start | bytes 6291460
  78.4 4.7 %collective-permute-start.3 = (bf16[1024,512]{0,1:T(8,128)(2,1)S(1)}, bf16[1024,512]{0,1:T(8,128)(2,1)S(1)}, u32[]{:S(2)}, u32[]{:S(2)}) collective-permute-start(bf16[1024,512]{0,1:T(8,128)(2,1)S(1)} %multiply_convert_fusion), channel_id=1, source_target_pairs={{0,1},{1,0},{2,3},{3,2},{4,5},{5,4},{6,7},{7,6},{8,9},{9,8},{10,11... | collective-permute-start | bytes 3145736 | tf_op jit(solution)/shard_map/ppermute | solution.py:32
  88.1 23.4 %all-to-all-start.3 = ((bf16[4,8,128,128]{3,2,1,0:T(8,128)(2,1)}), bf16[4,8,128,128]{3,2,1,0:T(8,128)(2,1)S(1)}, u32[]{:S(2)}, u32[]{:S(2)}) async-start(bf16[4,8,128,128]{3,2,1,0:T(8,128)(2,1)} %broadcast_in_dim.34), calls=%async_computation.4 | async-start | bytes 2097152 | tf_op jit(solution)/shard_map/all_to_all | solution.py:26
  112.7 17.9 %all-to-all-start.4 = ((bf16[4,8,128,128]{3,2,1,0:T(8,128)(2,1)}), bf16[4,8,128,128]{3,2,1,0:T(8,128)(2,1)}, u32[]{:S(2)}, u32[]{:S(2)}) async-start(bf16[4,8,128,128]{3,2,1,0:T(8,128)(2,1)} %broadcast_in_dim.58), calls=%async_computation.5 | async-start | bytes 2097152 | tf_op jit(solution)/shard_map/all_to_all | solution.py:26
  117.0 54.6 %all-gather.7.cloned.1.call-start = ((), (), s32[]{:S(2)}) async-start(), calls=%async_computation.9 | async-start | bytes 1310720 | tf_op jit(solution)/shard_map/all_gather | solution.py:175
  132.1 12.4 %collective-permute-start.4 = (bf16[1024,128]{1,0:T(8,128)(2,1)}, bf16[1024,128]{1,0:T(8,128)(2,1)S(1)}, u32[]{:S(2)}, u32[]{:S(2)}) collective-permute-start(bf16[1024,128]{1,0:T(8,128)(2,1)} %reduce-scatter.2.cloned.1.call-done), channel_id=1, source_target_pairs={{0,64},{64,0},{1,65},{65,1},{2,66},{66,2},{3,67},{67,3},{4,68},{68... | collective-permute-start | bytes 786440 | tf_op jit(solution)/shard_map/ppermute | solution.py:32
  145.6 25.9 %all-to-all-start.5 = ((bf16[4,1024,128]{2,1,0:T(8,128)(2,1)}), bf16[4,1024,128]{2,1,0:T(8,128)(2,1)S(1)}, u32[]{:S(2)}, u32[]{:S(2)}) async-start(bf16[4,1024,128]{2,1,0:T(8,128)(2,1)} %broadcast_in_dim.62), calls=%async_computation.6 | async-start | bytes 2097152 | tf_op jit(solution)/shard_map/all_to_all | solution.py:26
  171.5 1.0 copy-start
  172.6 1.0 copy-start.1
  173.6 1.2 copy-start.2
Sparse Core Ops, SparseCore 0:
  30.9 37.9 all-gather.4
  85.8 43.3 reduce-scatter.1
  132.2 36.3 all-gather.6

commit v3 on v2

--- a/solution.py
+++ b/solution.py
@@ -104,14 +104,9 @@
     c = lax.axis_index("c")
     me = lax.axis_index(GROUP)
 
-    sent = tokens.reshape(own, nx, nc, rows)
-    sent = jnp.concatenate(
-        [jnp.where(c == 0, sent[:, :, 0], sent[:, :, 1]), jnp.where(c == 0, sent[:, :, 1], sent[:, :, 0])], axis=0
-    )
-    sent = sent.transpose(1, 0, 2)
-    mine = lax.all_to_all(sent, "x", split_axis=0, concat_axis=0, tiled=True)
-    pair = jnp.stack([mine[:, :own], swap(mine[:, own:], "c")])
-    left = lax.all_gather(pair, "y", axis=0, tiled=False)
+    sent = tokens.reshape(own, nx * nc, rows).transpose(1, 0, 2)
+    mine = lax.all_to_all(sent, ("x", "c"), split_axis=0, concat_axis=0, tiled=True)
+    left = lax.all_gather(mine, "y", axis=0, tiled=False)
 
     values = tokens.astype(jnp.float32)
     scale = lax.rsqrt(jnp.mean(values * values, axis=1, keepdims=True) + norm_eps)
@@ -124,7 +119,7 @@
         block = (master - learn_rate * momentum_rate * momentum).astype(jnp.bfloat16)
         return block.reshape(per_group, part_rows, columns)
 
-    scaled, pair = lax.optimization_barrier((scaled, pair))
+    scaled, mine = lax.optimization_barrier((scaled, mine))
     part = lax.all_to_all(scaled, "y", split_axis=0, concat_axis=0, tiled=True)
     before_other, part = lax.optimization_barrier((past(master[0, 0], momentum[0, 0]), part))
     before_other = swap(before_other, "h")
@@ -132,9 +127,13 @@
     right_own, before_other = lax.optimization_barrier((right_own, before_other))
     right_other = swap(right_own, "c")
     half = nl * columns
+
+    def by_core(ours, theirs):
+        return jnp.stack([jnp.where(c == 0, ours, theirs), jnp.where(c == 0, theirs, ours)], axis=1)
+
     halves = [
-        jnp.concatenate([right_own[..., :half], right_other[..., half:]]),
-        jnp.concatenate([right_own[..., half:], right_other[..., :half]]),
+        by_core(right_own[..., :half], right_other[..., half:]),
+        by_core(right_own[..., half:], right_other[..., :half]),
     ]
 
     owner_row = lax.dynamic_slice_in_dim(owner, lax.axis_index(DEV), 1, 0)[0]
@@ -149,7 +148,7 @@
     def product(right):
         out = lax.dot_general(
             left.reshape(-1, rows),
-            right.transpose(1, 0, 2, 3).reshape(-1, half),
+            right.transpose(2, 0, 1, 3, 4).reshape(-1, half),
             (((0,), (0,)), ((), ())),
             preferred_element_type=jnp.float32,
         )

time: 186 us -> 180 us (0.968)
  waiting for transfers between devices: 79.6 us -> 74 us
    all_to_all x1, starting transfers between devices: 4.84 us -> 10.3 us  [local(): lax.all_to_all(sent, ('x', 'c'), split_axis=0, concat_axis=0, tiled=True)]
    all_to_all x4, starting transfers between devices: 20.2 us -> 15.4 us  [spread(): lax.all_to_all(jnp.broadcast_to(block[None], (lax.axis_size(axis), *block...]
    all_to_all x1, waiting for transfers between devices: 12.2 us -> 9.98 us  [local(): part = lax.all_to_all(scaled, 'y', split_axis=0, concat_axis=0, tiled=True)]
    all_to_all x4, waiting for transfers between devices: 49.7 us -> 47.8 us  [spread(): lax.all_to_all(jnp.broadcast_to(block[None], (lax.axis_size(axis), *block...]
    unnamed x16 -> x17, local copies, waits for them, and re-layouts: 3.33 us -> 5.17 us
    ppermute x5 -> x4, waiting for transfers between devices: 12.3 us -> 10.8 us  [swap(): return lax.ppermute(block, axis, [(0, 1), (1, 0)])]
    ppermute x5 -> x4, starting transfers between devices: 30.8 us -> 30.5 us  [swap(): return lax.ppermute(block, axis, [(0, 1), (1, 0)])]
  transfers between devices with their start and end apart: 14 -> 13, of which waited for: 11 -> 9; matrix products, arithmetic and copies ran while one was open for 9% -> 9% of each run, Pallas kernels for 0% -> 0%
where the time goes in v3:
time: 180 us; the launch traced here: 179 us
  waiting for transfers between devices  74 us (41%)
  starting transfers between devices  59.8 us (33%)
  local copies, waits for them, and re-layouts  15.8 us (9%)
  between operations  14 us (8%)
  other arithmetic  7.85 us (4%)
  matrix products  4.13 us (2%)
  Pallas kernels  3.12 us (2%)
    all_to_all x4, waiting for transfers between devices, spread(): lax.all_to_all(jnp.broadcast_to(block[None], (lax.axis_size(axis), *block...  47.8 us
    ppermute x4, starting transfers between devices, swap(): return lax.ppermute(block, axis, [(0, 1), (1, 0)])  30.5 us
    all_to_all x4, starting transfers between devices, spread(): lax.all_to_all(jnp.broadcast_to(block[None], (lax.axis_size(axis), *block...  15.4 us
    ppermute x4, waiting for transfers between devices, swap(): return lax.ppermute(block, axis, [(0, 1), (1, 0)])  10.8 us
    all_to_all x1, starting transfers between devices, local(): lax.all_to_all(sent, ('x', 'c'), split_axis=0, concat_axis=0, tiled=True)  10.3 us
    all_to_all x1, waiting for transfers between devices, local(): part = lax.all_to_all(scaled, 'y', split_axis=0, concat_axis=0, tiled=True)  9.98 us
    all_to_all x1, waiting for transfers between devices, local(): lax.all_to_all(sent, ('x', 'c'), split_axis=0, concat_axis=0, tiled=True)  5.38 us
    unnamed x17, local copies, waits for them, and re-layouts  5.17 us
  transfers between devices with their start and end apart: 13, of which 9 were waited for; matrix products, arithmetic and copies ran while one was open for 9% of the time, Pallas kernels for 0%

profile of v3, /device:TPU:1, one launch (start us, length us, event | category | flops | bytes accessed | tf_op | source)
XLA Modules:
  0.0 178.7 jit_solution(16880466811973137568)
XLA Ops:
  7.2 1.1 copy.60
  8.3 0.9 copy.51
  9.2 10.3 %all-to-all-start = ((bf16[8,16,1024]{2,1,0:T(8,128)(2,1)}), bf16[8,16,1024]{2,1,0:T(8,128)(2,1)S(1)}, u32[]{:S(2)}, u32[]{:S(2)}) async-start(bf16[8,16,1024]{2,1,0:T(8,128)(2,1)} %copy.51), calls=%async_computation | async-start | bytes 524288 | tf_op jit(solution)/shard_map/all_to_all | solution.py:108
  19.5 1.1 multiply_reduce_fusion
  20.6 5.4 %all-to-all-done = bf16[8,16,1024]{2,1,0:T(8,128)(2,1)S(1)} async-done(((bf16[8,16,1024]{2,1,0:T(8,128)(2,1)}), bf16[8,16,1024]{2,1,0:T(8,128)(2,1)S(1)}, u32[]{:S(2)}, u32[]{:S(2)}) %all-to-all-start) | async-done | bytes 262176 | tf_op jit(solution)/shard_map/all_to_all | solution.py:108
  26.0 0.7 copy-done.6
  26.8 0.1 multiply_convert_fusion.2
  26.9 0.2 reshape.63
  27.2 0.1 fusion.1
  27.3 0.9 reshape.64
  28.2 3.4 %all-to-all-start.1 = ((bf16[8,16,1024]{2,1,0:T(8,128)(2,1)}), bf16[8,16,1024]{2,1,0:T(8,128)(2,1)S(1)}, u32[]{:S(2)}, u32[]{:S(2)}) async-start(bf16[8,16,1024]{2,1,0:T(8,128)(2,1)} %reshape.64), calls=%async_computation.1 | async-start | bytes 524288 | tf_op jit(solution)/shard_map/all_to_all | solution.py:123
  31.7 10.0 %all-to-all-done.1 = bf16[8,16,1024]{2,1,0:T(8,128)(2,1)S(1)} async-done(((bf16[8,16,1024]{2,1,0:T(8,128)(2,1)}), bf16[8,16,1024]{2,1,0:T(8,128)(2,1)S(1)}, u32[]{:S(2)}, u32[]{:S(2)}) %all-to-all-start.1) | async-done | bytes 262176 | tf_op jit(solution)/shard_map/all_to_all | solution.py:123
  41.7 1.1 broadcast_in_dim.32
  42.8 3.5 %all-to-all-start.2 = ((bf16[4,8,16,1024]{3,2,1,0:T(8,128)(2,1)}), bf16[4,8,16,1024]{3,2,1,0:T(8,128)(2,1)S(1)}, u32[]{:S(2)}, u32[]{:S(2)}) async-start(bf16[4,8,16,1024]{3,2,1,0:T(8,128)(2,1)} %broadcast_in_dim.32), calls=%async_computation.2 | async-start | bytes 2097152 | tf_op jit(solution)/shard_map/all_to_all | solution.py:26
  46.4 9.6 %collective-permute-start = (bf16[8,128,128]{2,0,1:T(8,128)(2,1)S(1)}, bf16[8,128,128]{2,0,1:T(8,128)(2,1)S(1)}, u32[]{:S(2)}, u32[]{:S(2)}) collective-permute-start(bf16[8,128,128]{2,0,1:T(8,128)(2,1)S(1)} %fusion.2), channel_id=1, source_target_pairs={{0,64},{64,0},{1,65},{65,1},{2,66},{66,2},{3,67},{67,3},{4,68},{68... | collective-permute-start | bytes 786440 | tf_op jit(solution)/shard_map/ppermute | solution.py:32
  56.0 3.8 %collective-permute-done = bf16[8,128,128]{2,0,1:T(8,128)(2,1)S(1)} collective-permute-done((bf16[8,128,128]{2,0,1:T(8,128)(2,1)S(1)}, bf16[8,128,128]{2,0,1:T(8,128)(2,1)S(1)}, u32[]{:S(2)}, u32[]{:S(2)}) %collective-permute-start) | collective-permute-done | bytes 262176 | tf_op jit(solution)/shard_map/ppermute | solution.py:32
  60.0 10.5 %collective-permute-start.1 = (bf16[4,8,16,1024]{3,2,0,1:T(8,128)(2,1)S(1)}, bf16[4,8,16,1024]{3,2,0,1:T(8,128)(2,1)}, u32[]{:S(2)}, u32[]{:S(2)}) collective-permute-start(bf16[4,8,16,1024]{3,2,0,1:T(8,128)(2,1)S(1)} %copy.52), channel_id=1, source_target_pairs={{0,1},{1,0},{2,3},{3,2},{4,5},{5,4},{6,7},{7,6},{8,9},{9,8},{10,11... | collective-permute-start | bytes 3145736 | tf_op jit(solution)/shard_map/ppermute | solution.py:32
  70.5 0.7 dynamic_slice.6
  71.2 1.7 collective-permute-done.1
  72.9 1.6 select_bitcast_fusion.3
  74.7 2.9 %fusion = bf16[1024,512]{0,1:T(8,128)(2,1)S(1)} fusion(bf16[1024,512]{1,0:T(8,128)(2,1)S(1)} %bitcast.60, bf16[1024,1024]{1,0:T(8,128)(2,1)} %bitcast.57, f32[1024]{0:T(1024)S(1)} %dynamic_slice.6), kind=kOutput, calls=%fused_computation.4 | convolution fusion | flops 1074790400 | bytes 4198400 | tf_op jit(solution)/shard_map/dot_general | solution.py:149
  77.6 2.4 %collective-permute-start.2 = (bf16[1024,512]{0,1:T(8,128)(2,1)S(1)}, bf16[1024,512]{0,1:T(8,128)(2,1)S(1)}, u32[]{:S(2)}, u32[]{:S(2)}) collective-permute-start(bf16[1024,512]{0,1:T(8,128)(2,1)S(1)} %fusion), channel_id=1, source_target_pairs={{0,1},{1,0},{2,3},{3,2},{4,5},{5,4},{6,7},{7,6},{8,9},{9,8},{10,11... | collective-permute-start | bytes 3145736 | tf_op jit(solution)/shard_map/ppermute | solution.py:32
  80.2 1.3 multiply_convert_fusion.1
  81.4 0.9 collective-permute-done.2
  82.3 0.2 pad_maximum_fusion
  82.5 2.4 %copy.57 = bf16[8,1024,128]{2,1,0:T(8,128)(2,1)} copy(bf16[8,1024,128]{1,2,0:T(8,128)(2,1)S(1)} %pad_maximum_fusion) | data formatting | bytes 4194304 | tf_op jit(solution)/shard_map/concatenate | solution.py:159
  84.9 1.1 convert_bitcast_fusion
  86.0 1.2 broadcast_in_dim.34
  87.2 4.1 %all-to-all-start.3 = ((bf16[4,8,128,128]{3,2,1,0:T(8,128)(2,1)}), bf16[4,8,128,128]{3,2,1,0:T(8,128)(2,1)S(1)}, u32[]{:S(2)}, u32[]{:S(2)}) async-start(bf16[4,8,128,128]{3,2,1,0:T(8,128)(2,1)} %broadcast_in_dim.34), calls=%async_computation.4 | async-start | bytes 2097152 | tf_op jit(solution)/shard_map/all_to_all | solution.py:26
  91.4 0.7 fusion.6
  92.1 13.8 %all-to-all-done.3 = bf16[4,8,128,128]{3,2,1,0:T(8,128)(2,1)S(1)} async-done(((bf16[4,8,128,128]{3,2,1,0:T(8,128)(2,1)}), bf16[4,8,128,128]{3,2,1,0:T(8,128)(2,1)S(1)}, u32[]{:S(2)}, u32[]{:S(2)}) %all-to-all-start.3) | async-done | bytes 1048608 | tf_op jit(solution)/shard_map/all_to_all | solution.py:26
  106.0 1.2 broadcast_in_dim.58
  107.2 4.2 %all-to-all-start.4 = ((bf16[4,8,128,128]{3,2,1,0:T(8,128)(2,1)}), bf16[4,8,128,128]{3,2,1,0:T(8,128)(2,1)}, u32[]{:S(2)}, u32[]{:S(2)}) async-start(bf16[4,8,128,128]{3,2,1,0:T(8,128)(2,1)} %broadcast_in_dim.58), calls=%async_computation.5 | async-start | bytes 2097152 | tf_op jit(solution)/shard_map/all_to_all | solution.py:26
  111.6 0.7 compare_bitcast_fusion
  112.3 0.2 select_reduce_fusion
  112.5 0.1 select_reduce_fusion.1.source_ref
  112.6 0.7 multiply_add_fusion.place_ref
  113.4 11.7 %all-to-all-done.4 = bf16[4,8,128,128]{3,2,1,0:T(8,128)(2,1)} async-done(((bf16[4,8,128,128]{3,2,1,0:T(8,128)(2,1)}), bf16[4,8,128,128]{3,2,1,0:T(8,128)(2,1)}, u32[]{:S(2)}, u32[]{:S(2)}) %all-to-all-start.4) | async-done | bytes 1048608 | tf_op jit(solution)/shard_map/all_to_all | solution.py:26
  125.1 1.4 pad_maximum_fusion.1
  126.5 8.0 %collective-permute-start.3 = (bf16[1024,128]{1,0:T(8,128)(2,1)}, bf16[1024,128]{1,0:T(8,128)(2,1)S(1)}, u32[]{:S(2)}, u32[]{:S(2)}) collective-permute-start(bf16[1024,128]{1,0:T(8,128)(2,1)} %reduce-scatter.2.cloned.1.call-done), channel_id=1, source_target_pairs={{0,64},{64,0},{1,65},{65,1},{2,66},{66,2},{3,67},{67,3},{4,68},{68... | collective-permute-start | bytes 786440 | tf_op jit(solution)/shard_map/ppermute | solution.py:32
  134.5 4.4 %collective-permute-done.3 = bf16[1024,128]{1,0:T(8,128)(2,1)S(1)} collective-permute-done((bf16[1024,128]{1,0:T(8,128)(2,1)}, bf16[1024,128]{1,0:T(8,128)(2,1)S(1)}, u32[]{:S(2)}, u32[]{:S(2)}) %collective-permute-start.3) | collective-permute-done | bytes 262176 | tf_op jit(solution)/shard_map/ppermute | solution.py:32
  138.9 1.1 broadcast_in_dim.62
  140.0 3.5 %all-to-all-start.5 = ((bf16[4,1024,128]{2,1,0:T(8,128)(2,1)}), bf16[4,1024,128]{2,1,0:T(8,128)(2,1)S(1)}, u32[]{:S(2)}, u32[]{:S(2)}) async-start(bf16[4,1024,128]{2,1,0:T(8,128)(2,1)} %broadcast_in_dim.62), calls=%async_computation.6 | async-start | bytes 2097152 | tf_op jit(solution)/shard_map/all_to_all | solution.py:26
  143.6 22.2 %all-to-all-done.5.other_ref = bf16[4,1024,128]{2,1,0:T(8,128)(2,1)S(1)} async-done(((bf16[4,1024,128]{2,1,0:T(8,128)(2,1)}), bf16[4,1024,128]{2,1,0:T(8,128)(2,1)S(1)}, u32[]{:S(2)}, u32[]{:S(2)}) %all-to-all-start.5) | async-done | bytes 1048608 | tf_op jit(solution)/shard_map/all_to_all | solution.py:26
  165.8 1.0 copy-done
  166.8 1.0 copy-done.1
  167.9 1.2 copy-done.2
  169.1 3.1 %finish.1 = (f32[8,16384]{1,0:T(8,128)}, f32[8,16384]{1,0:T(8,128)}, bf16[8192,128]{1,0:T(8,128)(2,1)}) custom-call(s32[1]{0:T(128)} %bitcast.h_ref, s32[8]{0:T(128)S(1)} %select_reduce_fusion.1.source_ref, s32[64]{0:T(128)S(1)} %multiply_add_fusion.place_ref, bf16[4,1024,128]{2,1,0:T(8,128)(2,1)S(1)} %bitcast.56, ...), custom_call_target="tpu_custom_call" | custom-call | flops 4000000 | bytes 8000000 | tf_op jit(solution)/shard_map/finish/pallas_call | solution.py:73
  (33 shorter events, 1.0 us)
Async XLA Ops:
  7.2 19.6 %copy-start.7 = (bf16[16,8192]{1,0:T(8,128)(2,1)S(1)}, bf16[16,8192]{1,0:T(8,128)(2,1)}, u32[]{:S(2)}) copy-start(bf16[16,8192]{1,0:T(8,128)(2,1)} %param.7) | copy-start | bytes 786436
  9.2 22.4 %copy-start.4 = (f32[1,1,8,16384]{3,2,1,0:T(8,128)S(1)}, f32[1,1,8,16384]{3,2,1,0:T(8,128)}, u32[]{:S(2)}) copy-start(f32[1,1,8,16384]{3,2,1,0:T(8,128)} %param.9) | copy-start | bytes 1572868
  9.2 22.4 %copy-start.5 = (f32[1,1,8,16384]{3,2,1,0:T(8,128)S(1)}, f32[1,1,8,16384]{3,2,1,0:T(8,128)}, u32[]{:S(2)}) copy-start(f32[1,1,8,16384]{3,2,1,0:T(8,128)} %param.10) | copy-start | bytes 1572868
  9.2 16.8 %all-to-all-start = ((bf16[8,16,1024]{2,1,0:T(8,128)(2,1)}), bf16[8,16,1024]{2,1,0:T(8,128)(2,1)S(1)}, u32[]{:S(2)}, u32[]{:S(2)}) async-start(bf16[8,16,1024]{2,1,0:T(8,128)(2,1)} %copy.51), calls=%async_computation | async-start | bytes 524288 | tf_op jit(solution)/shard_map/all_to_all | solution.py:108
  19.5 55.2 %all-gather.5.cloned.1.call-start = ((), (), s32[]{:S(2)}) async-start(), calls=%async_computation.8 | async-start | bytes 2359296 | tf_op jit(solution)/shard_map/all_gather | solution.py:109
  26.0 0.7 copy-start.6
  28.2 13.5 %all-to-all-start.1 = ((bf16[8,16,1024]{2,1,0:T(8,128)(2,1)}), bf16[8,16,1024]{2,1,0:T(8,128)(2,1)S(1)}, u32[]{:S(2)}, u32[]{:S(2)}) async-start(bf16[8,16,1024]{2,1,0:T(8,128)(2,1)} %reshape.64), calls=%async_computation.1 | async-start | bytes 524288 | tf_op jit(solution)/shard_map/all_to_all | solution.py:123
  42.8 17.1 %all-to-all-start.2 = ((bf16[4,8,16,1024]{3,2,1,0:T(8,128)(2,1)}), bf16[4,8,16,1024]{3,2,1,0:T(8,128)(2,1)S(1)}, u32[]{:S(2)}, u32[]{:S(2)}) async-start(bf16[4,8,16,1024]{3,2,1,0:T(8,128)(2,1)} %broadcast_in_dim.32), calls=%async_computation.2 | async-start | bytes 2097152 | tf_op jit(solution)/shard_map/all_to_all | solution.py:26
  46.3 80.2 %reduce-scatter.2.cloned.1.call-start = ((), (), s32[]{:S(2)}) async-start(), calls=%async_computation.7 | async-start | bytes 2359296 | tf_op jit(solution)/shard_map/reduce_scatter | solution.py:161
  46.4 13.5 %collective-permute-start = (bf16[8,128,128]{2,0,1:T(8,128)(2,1)S(1)}, bf16[8,128,128]{2,0,1:T(8,128)(2,1)S(1)}, u32[]{:S(2)}, u32[]{:S(2)}) collective-permute-start(bf16[8,128,128]{2,0,1:T(8,128)(2,1)S(1)} %fusion.2), channel_id=1, source_target_pairs={{0,64},{64,0},{1,65},{65,1},{2,66},{66,2},{3,67},{67,3},{4,68},{68... | collective-permute-start | bytes 786440 | tf_op jit(solution)/shard_map/ppermute | solution.py:32
  60.0 12.9 %collective-permute-start.1 = (bf16[4,8,16,1024]{3,2,0,1:T(8,128)(2,1)S(1)}, bf16[4,8,16,1024]{3,2,0,1:T(8,128)(2,1)}, u32[]{:S(2)}, u32[]{:S(2)}) collective-permute-start(bf16[4,8,16,1024]{3,2,0,1:T(8,128)(2,1)S(1)} %copy.52), channel_id=1, source_target_pairs={{0,1},{1,0},{2,3},{3,2},{4,5},{5,4},{6,7},{7,6},{8,9},{9,8},{10,11... | collective-permute-start | bytes 3145736 | tf_op jit(solution)/shard_map/ppermute | solution.py:32
  77.6 2.5 %copy-start.3 = (bf16[64,16,1024]{2,1,0:T(8,128)(2,1)S(1)}, bf16[64,16,1024]{2,1,0:T(8,128)(2,1)}, u32[]{:S(2)}) copy-start(bf16[64,16,1024]{2,1,0:T(8,128)(2,1)} %all-gather.5.cloned.1.call-done) | copy-start | bytes 6291460
  77.6 4.7 %collective-permute-start.2 = (bf16[1024,512]{0,1:T(8,128)(2,1)S(1)}, bf16[1024,512]{0,1:T(8,128)(2,1)S(1)}, u32[]{:S(2)}, u32[]{:S(2)}) collective-permute-start(bf16[1024,512]{0,1:T(8,128)(2,1)S(1)} %fusion), channel_id=1, source_target_pairs={{0,1},{1,0},{2,3},{3,2},{4,5},{5,4},{6,7},{7,6},{8,9},{9,8},{10,11... | collective-permute-start | bytes 3145736 | tf_op jit(solution)/shard_map/ppermute | solution.py:32
  87.2 18.7 %all-to-all-start.3 = ((bf16[4,8,128,128]{3,2,1,0:T(8,128)(2,1)}), bf16[4,8,128,128]{3,2,1,0:T(8,128)(2,1)S(1)}, u32[]{:S(2)}, u32[]{:S(2)}) async-start(bf16[4,8,128,128]{3,2,1,0:T(8,128)(2,1)} %broadcast_in_dim.34), calls=%async_computation.4 | async-start | bytes 2097152 | tf_op jit(solution)/shard_map/all_to_all | solution.py:26
  107.2 17.9 %all-to-all-start.4 = ((bf16[4,8,128,128]{3,2,1,0:T(8,128)(2,1)}), bf16[4,8,128,128]{3,2,1,0:T(8,128)(2,1)}, u32[]{:S(2)}, u32[]{:S(2)}) async-start(bf16[4,8,128,128]{3,2,1,0:T(8,128)(2,1)} %broadcast_in_dim.58), calls=%async_computation.5 | async-start | bytes 2097152 | tf_op jit(solution)/shard_map/all_to_all | solution.py:26
  111.4 54.3 %all-gather.7.cloned.1.call-start = ((), (), s32[]{:S(2)}) async-start(), calls=%async_computation.9 | async-start | bytes 1310720 | tf_op jit(solution)/shard_map/all_gather | solution.py:174
  126.5 12.4 %collective-permute-start.3 = (bf16[1024,128]{1,0:T(8,128)(2,1)}, bf16[1024,128]{1,0:T(8,128)(2,1)S(1)}, u32[]{:S(2)}, u32[]{:S(2)}) collective-permute-start(bf16[1024,128]{1,0:T(8,128)(2,1)} %reduce-scatter.2.cloned.1.call-done), channel_id=1, source_target_pairs={{0,64},{64,0},{1,65},{65,1},{2,66},{66,2},{3,67},{67,3},{4,68},{68... | collective-permute-start | bytes 786440 | tf_op jit(solution)/shard_map/ppermute | solution.py:32
  140.0 25.7 %all-to-all-start.5 = ((bf16[4,1024,128]{2,1,0:T(8,128)(2,1)}), bf16[4,1024,128]{2,1,0:T(8,128)(2,1)S(1)}, u32[]{:S(2)}, u32[]{:S(2)}) async-start(bf16[4,1024,128]{2,1,0:T(8,128)(2,1)} %broadcast_in_dim.62), calls=%async_computation.6 | async-start | bytes 2097152 | tf_op jit(solution)/shard_map/all_to_all | solution.py:26
  165.8 1.0 copy-start
  166.8 1.0 copy-start.1
  167.8 1.2 copy-start.2
Sparse Core Ops, SparseCore 0:
  26.9 38.6 all-gather.4
  85.0 38.7 reduce-scatter.1
  126.7 35.9 all-gather.6

commit v4 on v3

--- a/solution.py
+++ b/solution.py
@@ -138,17 +138,17 @@
 
     owner_row = lax.dynamic_slice_in_dim(owner, lax.axis_index(DEV), 1, 0)[0]
     rank = slot_table(owner_row, groups)
-    place = (jnp.where(owner_row % nh == h, 0, nx) + owner_row // nh) * per_group + rank
+    place = (owner_row // nh * nh + jnp.where(owner_row % nh == h, 0, 1)) * per_group + rank
     slots = jnp.arange(per_group, dtype=jnp.int32)
     hit = (owner_row[None, :] == me) & (rank[None, :] == slots[:, None])
     source = jnp.sum(jnp.where(hit, jnp.arange(part_count, dtype=jnp.int32)[None, :], 0), axis=1)
 
-    weight = lax.dynamic_slice_in_dim(gain, (lax.axis_index("x") * nc + c) * rows, rows, 0)[:, None]
+    weight = lax.dynamic_slice_in_dim(gain, (lax.axis_index("x") * nc + c) * rows, rows, 0)[None]
 
     def product(right):
         out = lax.dot_general(
+            right.transpose(2, 0, 1, 3, 4).reshape(-1, half),
             left.reshape(-1, rows),
-            right.transpose(2, 0, 1, 3, 4).reshape(-1, half),
             (((0,), (0,)), ((), ())),
             preferred_element_type=jnp.float32,
         )
@@ -156,15 +156,12 @@
 
     came = swap(product(halves[1]), "c")
     keep = product(halves[0])
-    both = jnp.concatenate([block.reshape(rows, nl, columns).transpose(1, 0, 2) for block in (keep, came)])
-    both = both.reshape(nh * nl * rows, columns)
-    summed = lax.psum_scatter(both, ("h", "l"), scatter_dimension=0, tiled=True)
+    both = jnp.concatenate([keep, came])
+    summed = lax.psum_scatter(both, ("h", "l"), scatter_dimension=0, tiled=True).T
 
     base_master, base_momentum, _ = lax.optimization_barrier((master[0, 0], momentum[0, 0], came))
-    before_own = spread(past(base_master, base_momentum), "x")
-    before_own, before_other = lax.optimization_barrier((before_own, before_other))
-    before_other = spread(before_other, "x")
-    pulled = jnp.concatenate([before_own, before_other]).reshape(part_count, part_rows, columns)
+    both_h = jnp.stack([past(base_master, base_momentum), before_other])
+    pulled = spread(both_h, "x").reshape(part_count, part_rows, columns)
     base_master = base_master - learn_rate * momentum_rate * base_momentum
     base_momentum = momentum_rate * base_momentum
     summed, pulled, place, source, base_master, base_momentum = lax.optimization_barrier(

time: 180 us -> 179 us (level)
  starting transfers between devices: 59.8 us -> 52.4 us
  waiting for transfers between devices: 74 us -> 80.9 us
    all_to_all x4 -> x3, waiting for transfers between devices: 47.8 us -> 26.6 us  [spread(): lax.all_to_all(jnp.broadcast_to(block[None], (lax.axis_size(axis), *block...]
    all_gather x1, waiting for transfers between devices: 0.01 us -> 14.5 us  [local(): full_own = lax.all_gather(summed, 'x', axis=0, tiled=False)]
    ppermute x4, waiting for transfers between devices: 10.8 us -> 18 us  [swap(): return lax.ppermute(block, axis, [(0, 1), (1, 0)])]
    reduce_scatter x1, waiting for transfers between devices: 0.02 us -> 6.29 us  [local(): lax.psum_scatter(both, ('h', 'l'), scatter_dimension=0, tiled=True)]
    all_to_all x4 -> x3, starting transfers between devices: 15.4 us -> 11.2 us  [spread(): lax.all_to_all(jnp.broadcast_to(block[None], (lax.axis_size(axis), *block...]
    ppermute x4, starting transfers between devices: 30.5 us -> 27.4 us  [swap(): return lax.ppermute(block, axis, [(0, 1), (1, 0)])]
    concatenate x1 -> x0, local copies, waits for them, and re-layouts: 2.38 us -> none  [local(): jnp.concatenate([block.reshape(rows, nl, columns).transpose(1, 0, 2) for...]
    all_gather x0 -> x1, local copies, waits for them, and re-layouts: none -> 2.26 us  [local(): full_own = lax.all_gather(summed, 'x', axis=0, tiled=False)]
  transfers between devices with their start and end apart: 13 -> 12, of which waited for: 9 -> 10; matrix products, arithmetic and copies ran while one was open for 9% -> 10% of each run, Pallas kernels for 0% -> 0%
where the time goes in v4:
time: 179 us; the launch traced here: 178 us
  waiting for transfers between devices  80.9 us (45%)
  starting transfers between devices  52.4 us (29%)
  local copies, waits for them, and re-layouts  15.4 us (9%)
  between operations  14 us (8%)
  other arithmetic  7.8 us (4%)
  matrix products  4.15 us (2%)
  Pallas kernels  3.14 us (2%)
    ppermute x4, starting transfers between devices, swap(): return lax.ppermute(block, axis, [(0, 1), (1, 0)])  27.4 us
    all_to_all x3, waiting for transfers between devices, spread(): lax.all_to_all(jnp.broadcast_to(block[None], (lax.axis_size(axis), *block...  26.6 us
    ppermute x4, waiting for transfers between devices, swap(): return lax.ppermute(block, axis, [(0, 1), (1, 0)])  18 us
    all_gather x1, waiting for transfers between devices, local(): full_own = lax.all_gather(summed, 'x', axis=0, tiled=False)  14.5 us
    all_to_all x3, starting transfers between devices, spread(): lax.all_to_all(jnp.broadcast_to(block[None], (lax.axis_size(axis), *block...  11.2 us
    all_to_all x1, starting transfers between devices, local(): lax.all_to_all(sent, ('x', 'c'), split_axis=0, concat_axis=0, tiled=True)  10.3 us
    all_to_all x1, waiting for transfers between devices, local(): part = lax.all_to_all(scaled, 'y', split_axis=0, concat_axis=0, tiled=True)  9.98 us
    reduce_scatter x1, waiting for transfers between devices, local(): lax.psum_scatter(both, ('h', 'l'), scatter_dimension=0, tiled=True)  6.29 us
  transfers between devices with their start and end apart: 12, of which 10 were waited for; matrix products, arithmetic and copies ran while one was open for 10% of the time, Pallas kernels for 0%

profile of v4, /device:TPU:1, one launch (start us, length us, event | category | flops | bytes accessed | tf_op | source)
XLA Modules:
  0.0 177.7 jit_solution(3015384916738152938)
XLA Ops:
  7.2 1.1 copy.60
  8.3 0.9 copy.51
  9.2 10.3 %all-to-all-start = ((bf16[8,16,1024]{2,1,0:T(8,128)(2,1)}), bf16[8,16,1024]{2,1,0:T(8,128)(2,1)S(1)}, u32[]{:S(2)}, u32[]{:S(2)}) async-start(bf16[8,16,1024]{2,1,0:T(8,128)(2,1)} %copy.51), calls=%async_computation | async-start | bytes 524288 | tf_op jit(solution)/shard_map/all_to_all | solution.py:108
  19.5 1.1 multiply_reduce_fusion
  20.6 5.4 %all-to-all-done = bf16[8,16,1024]{2,1,0:T(8,128)(2,1)S(1)} async-done(((bf16[8,16,1024]{2,1,0:T(8,128)(2,1)}), bf16[8,16,1024]{2,1,0:T(8,128)(2,1)S(1)}, u32[]{:S(2)}, u32[]{:S(2)}) %all-to-all-start) | async-done | bytes 262176 | tf_op jit(solution)/shard_map/all_to_all | solution.py:108
  26.0 0.7 copy-done.6
  26.8 0.1 multiply_convert_fusion.2
  26.9 0.2 reshape.53
  27.2 0.1 fusion
  27.3 0.9 reshape.54
  28.2 3.4 %all-to-all-start.1 = ((bf16[8,16,1024]{2,1,0:T(8,128)(2,1)}), bf16[8,16,1024]{2,1,0:T(8,128)(2,1)S(1)}, u32[]{:S(2)}, u32[]{:S(2)}) async-start(bf16[8,16,1024]{2,1,0:T(8,128)(2,1)} %reshape.54), calls=%async_computation.1 | async-start | bytes 524288 | tf_op jit(solution)/shard_map/all_to_all | solution.py:123
  31.7 10.0 %all-to-all-done.1 = bf16[8,16,1024]{2,1,0:T(8,128)(2,1)S(1)} async-done(((bf16[8,16,1024]{2,1,0:T(8,128)(2,1)}), bf16[8,16,1024]{2,1,0:T(8,128)(2,1)S(1)}, u32[]{:S(2)}, u32[]{:S(2)}) %all-to-all-start.1) | async-done | bytes 262176 | tf_op jit(solution)/shard_map/all_to_all | solution.py:123
  41.7 1.1 broadcast_in_dim.26
  42.8 3.5 %all-to-all-start.2 = ((bf16[4,8,16,1024]{3,2,1,0:T(8,128)(2,1)}), bf16[4,8,16,1024]{3,2,1,0:T(8,128)(2,1)S(1)}, u32[]{:S(2)}, u32[]{:S(2)}) async-start(bf16[4,8,16,1024]{3,2,1,0:T(8,128)(2,1)} %broadcast_in_dim.26), calls=%async_computation.2 | async-start | bytes 2097152 | tf_op jit(solution)/shard_map/all_to_all | solution.py:26
  46.4 9.6 %collective-permute-start = (bf16[8,128,128]{2,0,1:T(8,128)(2,1)S(1)}, bf16[8,128,128]{2,0,1:T(8,128)(2,1)S(1)}, u32[]{:S(2)}, u32[]{:S(2)}) collective-permute-start(bf16[8,128,128]{2,0,1:T(8,128)(2,1)S(1)} %fusion.1), channel_id=1, source_target_pairs={{0,64},{64,0},{1,65},{65,1},{2,66},{66,2},{3,67},{67,3},{4,68},{68... | collective-permute-start | bytes 786440 | tf_op jit(solution)/shard_map/ppermute | solution.py:32
  56.0 3.8 %collective-permute-done = bf16[8,128,128]{2,0,1:T(8,128)(2,1)S(1)} collective-permute-done((bf16[8,128,128]{2,0,1:T(8,128)(2,1)S(1)}, bf16[8,128,128]{2,0,1:T(8,128)(2,1)S(1)}, u32[]{:S(2)}, u32[]{:S(2)}) %collective-permute-start) | collective-permute-done | bytes 262176 | tf_op jit(solution)/shard_map/ppermute | solution.py:32
  59.9 0.1 copy.52
  60.0 10.5 %collective-permute-start.1 = (bf16[4,8,16,1024]{3,2,0,1:T(8,128)(2,1)S(1)}, bf16[4,8,16,1024]{3,2,0,1:T(8,128)(2,1)}, u32[]{:S(2)}, u32[]{:S(2)}) collective-permute-start(bf16[4,8,16,1024]{3,2,0,1:T(8,128)(2,1)S(1)} %copy.52), channel_id=1, source_target_pairs={{0,1},{1,0},{2,3},{3,2},{4,5},{5,4},{6,7},{7,6},{8,9},{9,8},{10,11... | collective-permute-start | bytes 3145736 | tf_op jit(solution)/shard_map/ppermute | solution.py:32
  70.5 0.7 dynamic_slice.6
  71.2 1.7 collective-permute-done.1
  72.9 1.6 select_bitcast_fusion.3
  74.7 2.9 %multiply_convert_fusion = bf16[512,1024]{1,0:T(8,128)(2,1)S(1)} fusion(bf16[1024,512]{1,0:T(8,128)(2,1)S(1)} %bitcast.50, bf16[1024,1024]{1,0:T(8,128)(2,1)} %bitcast.48, f32[1024]{0:T(1024)S(1)} %dynamic_slice.6), kind=kOutput, calls=%fused_computation.1 | convolution fusion | flops 1074790400 | bytes 4198400 | tf_op jit(solution)/shard_map/dot_general | solution.py:149
  77.6 2.4 %collective-permute-start.2 = (bf16[512,1024]{1,0:T(8,128)(2,1)S(1)}, bf16[512,1024]{1,0:T(8,128)(2,1)S(1)}, u32[]{:S(2)}, u32[]{:S(2)}) collective-permute-start(bf16[512,1024]{1,0:T(8,128)(2,1)S(1)} %multiply_convert_fusion), channel_id=1, source_target_pairs={{0,1},{1,0},{2,3},{3,2},{4,5},{5,4},{6,7},{7,6},{8,9},{9,8},{10,11... | collective-permute-start | bytes 3145736 | tf_op jit(solution)/shard_map/ppermute | solution.py:32
  80.2 1.3 multiply_convert_fusion.1
  81.5 0.8 collective-permute-done.2
  82.3 1.5 pad_maximum_fusion
  83.8 1.1 convert_bitcast_fusion
  85.1 1.9 %broadcast_in_dim.27 = bf16[4,2,8,128,128]{4,3,2,1,0:T(8,128)(2,1)} broadcast(bf16[2,8,128,128]{3,2,1,0:T(8,128)(2,1)S(1)} %copy.57), dimensions={1,2,3,4} | broadcast | bytes 2621440 | tf_op jit(solution)/shard_map/broadcast_in_dim | solution.py:27
  87.0 4.1 %all-to-all-start.3 = ((bf16[4,2,8,128,128]{4,3,2,1,0:T(8,128)(2,1)}), bf16[4,2,8,128,128]{4,3,2,1,0:T(8,128)(2,1)S(1)}, u32[]{:S(2)}, u32[]{:S(2)}) async-start(bf16[4,2,8,128,128]{4,3,2,1,0:T(8,128)(2,1)} %broadcast_in_dim.27), calls=%async_computation.4 | async-start | bytes 4194304 | tf_op jit(solution)/shard_map/all_to_all | solution.py:26
  91.1 0.7 fusion.5
  92.0 0.7 compare_bitcast_fusion
  92.7 0.2 select_reduce_fusion
  92.9 0.1 select_reduce_fusion.1.source_ref
  93.0 0.7 multiply_add_fusion.place_ref
  93.7 23.2 %all-to-all-done.3 = bf16[4,2,8,128,128]{4,3,2,1,0:T(8,128)(2,1)S(1)} async-done(((bf16[4,2,8,128,128]{4,3,2,1,0:T(8,128)(2,1)}), bf16[4,2,8,128,128]{4,3,2,1,0:T(8,128)(2,1)S(1)}, u32[]{:S(2)}, u32[]{:S(2)}) %all-to-all-start.3) | async-done | bytes 2097184 | tf_op jit(solution)/shard_map/all_to_all | solution.py:26
  116.9 6.3 %reduce-scatter.2.cloned.1.call-done = bf16[128,1024]{1,0:T(8,128)(2,1)} async-done(((bf16[1024,1024]{1,0:T(8,128)(2,1)}), bf16[128,1024]{1,0:T(8,128)(2,1)}) %reduce-scatter.2.cloned.1.call-update) | async-done | bytes 262160 | tf_op jit(solution)/shard_map/reduce_scatter | solution.py:160
  123.2 4.8 %collective-permute-start.3 = (bf16[1024,128]{0,1:T(8,128)(2,1)}, bf16[1024,128]{0,1:T(8,128)(2,1)S(1)}, u32[]{:S(2)}, u32[]{:S(2)}) collective-permute-start(bf16[1024,128]{0,1:T(8,128)(2,1)} %bitcast.57), channel_id=1, source_target_pairs={{0,64},{64,0},{1,65},{65,1},{2,66},{66,2},{3,67},{67,3},{4,68},{68... | collective-permute-start | bytes 786440 | tf_op jit(solution)/shard_map/ppermute | solution.py:32
  128.0 11.6 %collective-permute-done.3 = bf16[1024,128]{0,1:T(8,128)(2,1)S(1)} collective-permute-done((bf16[1024,128]{0,1:T(8,128)(2,1)}, bf16[1024,128]{0,1:T(8,128)(2,1)S(1)}, u32[]{:S(2)}, u32[]{:S(2)}) %collective-permute-start.3) | collective-permute-done | bytes 262176 | tf_op jit(solution)/shard_map/ppermute | solution.py:32
  139.7 0.2 copy.59
  139.8 1.1 broadcast_in_dim.30
  141.0 3.5 %all-to-all-start.4 = ((bf16[4,1024,128]{2,1,0:T(8,128)(2,1)}), bf16[4,1024,128]{2,1,0:T(8,128)(2,1)S(1)}, u32[]{:S(2)}, u32[]{:S(2)}) async-start(bf16[4,1024,128]{2,1,0:T(8,128)(2,1)} %broadcast_in_dim.30), calls=%async_computation.5 | async-start | bytes 2097152 | tf_op jit(solution)/shard_map/all_to_all | solution.py:26
  144.5 14.5 %all-gather.7.cloned.1.call-done = bf16[4096,128]{0,1:T(8,128)(2,1)} async-done(((bf16[1024,128]{0,1:T(8,128)(2,1)}), bf16[4096,128]{0,1:T(8,128)(2,1)}) %all-gather.7.cloned.1.call-update) | async-done | bytes 1048592 | tf_op jit(solution)/shard_map/all_gather | solution.py:171
  159.0 2.3 %copy.58 = bf16[4096,128]{1,0:T(8,128)(2,1)} copy(bf16[4096,128]{0,1:T(8,128)(2,1)} %all-gather.7.cloned.1.call-done) | data formatting | bytes 2097152 | tf_op jit(solution)/shard_map/all_gather | solution.py:171
  161.3 3.5 %all-to-all-done.4.other_ref = bf16[4,1024,128]{2,1,0:T(8,128)(2,1)S(1)} async-done(((bf16[4,1024,128]{2,1,0:T(8,128)(2,1)}), bf16[4,1024,128]{2,1,0:T(8,128)(2,1)S(1)}, u32[]{:S(2)}, u32[]{:S(2)}) %all-to-all-start.4) | async-done | bytes 1048608 | tf_op jit(solution)/shard_map/all_to_all | solution.py:26
  164.7 1.2 copy-done
  165.9 1.0 copy-done.1
  167.0 1.0 copy-done.2
  168.0 3.1 %finish.1 = (f32[8,16384]{1,0:T(8,128)}, f32[8,16384]{1,0:T(8,128)}, bf16[8192,128]{1,0:T(8,128)(2,1)}) custom-call(s32[1]{0:T(128)} %bitcast.h_ref, s32[8]{0:T(128)S(1)} %select_reduce_fusion.1.source_ref, s32[64]{0:T(128)S(1)} %multiply_add_fusion.place_ref, bf16[4,1024,128]{2,1,0:T(8,128)(2,1)S(1)} %bitcast.47, ...), custom_call_target="tpu_custom_call" | custom-call | flops 4000000 | bytes 8000000 | tf_op jit(solution)/shard_map/finish/pallas_call | solution.py:73
  (30 shorter events, 0.9 us)
Async XLA Ops:
  7.2 19.6 %copy-start.7 = (bf16[16,8192]{1,0:T(8,128)(2,1)S(1)}, bf16[16,8192]{1,0:T(8,128)(2,1)}, u32[]{:S(2)}) copy-start(bf16[16,8192]{1,0:T(8,128)(2,1)} %param.7) | copy-start | bytes 786436
  9.2 22.4 %copy-start.4 = (f32[1,1,8,16384]{3,2,1,0:T(8,128)S(1)}, f32[1,1,8,16384]{3,2,1,0:T(8,128)}, u32[]{:S(2)}) copy-start(f32[1,1,8,16384]{3,2,1,0:T(8,128)} %param.9) | copy-start | bytes 1572868
  9.2 22.4 %copy-start.5 = (f32[1,1,8,16384]{3,2,1,0:T(8,128)S(1)}, f32[1,1,8,16384]{3,2,1,0:T(8,128)}, u32[]{:S(2)}) copy-start(f32[1,1,8,16384]{3,2,1,0:T(8,128)} %param.10) | copy-start | bytes 1572868
  9.2 16.8 %all-to-all-start = ((bf16[8,16,1024]{2,1,0:T(8,128)(2,1)}), bf16[8,16,1024]{2,1,0:T(8,128)(2,1)S(1)}, u32[]{:S(2)}, u32[]{:S(2)}) async-start(bf16[8,16,1024]{2,1,0:T(8,128)(2,1)} %copy.51), calls=%async_computation | async-start | bytes 524288 | tf_op jit(solution)/shard_map/all_to_all | solution.py:108
  19.5 55.2 %all-gather.5.cloned.1.call-start = ((), (), s32[]{:S(2)}) async-start(), calls=%async_computation.7 | async-start | bytes 2359296 | tf_op jit(solution)/shard_map/all_gather | solution.py:109
  26.0 0.7 copy-start.6
  28.2 13.5 %all-to-all-start.1 = ((bf16[8,16,1024]{2,1,0:T(8,128)(2,1)}), bf16[8,16,1024]{2,1,0:T(8,128)(2,1)S(1)}, u32[]{:S(2)}, u32[]{:S(2)}) async-start(bf16[8,16,1024]{2,1,0:T(8,128)(2,1)} %reshape.54), calls=%async_computation.1 | async-start | bytes 524288 | tf_op jit(solution)/shard_map/all_to_all | solution.py:123
  42.8 17.1 %all-to-all-start.2 = ((bf16[4,8,16,1024]{3,2,1,0:T(8,128)(2,1)}), bf16[4,8,16,1024]{3,2,1,0:T(8,128)(2,1)S(1)}, u32[]{:S(2)}, u32[]{:S(2)}) async-start(bf16[4,8,16,1024]{3,2,1,0:T(8,128)(2,1)} %broadcast_in_dim.26), calls=%async_computation.2 | async-start | bytes 2097152 | tf_op jit(solution)/shard_map/all_to_all | solution.py:26
  46.3 76.8 %reduce-scatter.2.cloned.1.call-start = ((), (), s32[]{:S(2)}) async-start(), calls=%async_computation.6 | async-start | bytes 2359296 | tf_op jit(solution)/shard_map/reduce_scatter | solution.py:160
  46.4 13.5 %collective-permute-start = (bf16[8,128,128]{2,0,1:T(8,128)(2,1)S(1)}, bf16[8,128,128]{2,0,1:T(8,128)(2,1)S(1)}, u32[]{:S(2)}, u32[]{:S(2)}) collective-permute-start(bf16[8,128,128]{2,0,1:T(8,128)(2,1)S(1)} %fusion.1), channel_id=1, source_target_pairs={{0,64},{64,0},{1,65},{65,1},{2,66},{66,2},{3,67},{67,3},{4,68},{68... | collective-permute-start | bytes 786440 | tf_op jit(solution)/shard_map/ppermute | solution.py:32
  60.0 12.9 %collective-permute-start.1 = (bf16[4,8,16,1024]{3,2,0,1:T(8,128)(2,1)S(1)}, bf16[4,8,16,1024]{3,2,0,1:T(8,128)(2,1)}, u32[]{:S(2)}, u32[]{:S(2)}) collective-permute-start(bf16[4,8,16,1024]{3,2,0,1:T(8,128)(2,1)S(1)} %copy.52), channel_id=1, source_target_pairs={{0,1},{1,0},{2,3},{3,2},{4,5},{5,4},{6,7},{7,6},{8,9},{9,8},{10,11... | collective-permute-start | bytes 3145736 | tf_op jit(solution)/shard_map/ppermute | solution.py:32
  77.6 2.5 %copy-start.3 = (bf16[64,16,1024]{2,1,0:T(8,128)(2,1)S(1)}, bf16[64,16,1024]{2,1,0:T(8,128)(2,1)}, u32[]{:S(2)}) copy-start(bf16[64,16,1024]{2,1,0:T(8,128)(2,1)} %all-gather.5.cloned.1.call-done) | copy-start | bytes 6291460
  77.6 4.7 %collective-permute-start.2 = (bf16[512,1024]{1,0:T(8,128)(2,1)S(1)}, bf16[512,1024]{1,0:T(8,128)(2,1)S(1)}, u32[]{:S(2)}, u32[]{:S(2)}) collective-permute-start(bf16[512,1024]{1,0:T(8,128)(2,1)S(1)} %multiply_convert_fusion), channel_id=1, source_target_pairs={{0,1},{1,0},{2,3},{3,2},{4,5},{5,4},{6,7},{7,6},{8,9},{9,8},{10,11... | collective-permute-start | bytes 3145736 | tf_op jit(solution)/shard_map/ppermute | solution.py:32
  87.0 29.9 %all-to-all-start.3 = ((bf16[4,2,8,128,128]{4,3,2,1,0:T(8,128)(2,1)}), bf16[4,2,8,128,128]{4,3,2,1,0:T(8,128)(2,1)S(1)}, u32[]{:S(2)}, u32[]{:S(2)}) async-start(bf16[4,2,8,128,128]{4,3,2,1,0:T(8,128)(2,1)} %broadcast_in_dim.27), calls=%async_computation.4 | async-start | bytes 4194304 | tf_op jit(solution)/shard_map/all_to_all | solution.py:26
  91.1 67.9 %all-gather.7.cloned.1.call-start = ((), (), s32[]{:S(2)}) async-start(), calls=%async_computation.8 | async-start | bytes 1310720 | tf_op jit(solution)/shard_map/all_gather | solution.py:171
  123.2 16.5 %collective-permute-start.3 = (bf16[1024,128]{0,1:T(8,128)(2,1)}, bf16[1024,128]{0,1:T(8,128)(2,1)S(1)}, u32[]{:S(2)}, u32[]{:S(2)}) collective-permute-start(bf16[1024,128]{0,1:T(8,128)(2,1)} %bitcast.57), channel_id=1, source_target_pairs={{0,64},{64,0},{1,65},{65,1},{2,66},{66,2},{3,67},{67,3},{4,68},{68... | collective-permute-start | bytes 786440 | tf_op jit(solution)/shard_map/ppermute | solution.py:32
  141.0 23.7 %all-to-all-start.4 = ((bf16[4,1024,128]{2,1,0:T(8,128)(2,1)}), bf16[4,1024,128]{2,1,0:T(8,128)(2,1)S(1)}, u32[]{:S(2)}, u32[]{:S(2)}) async-start(bf16[4,1024,128]{2,1,0:T(8,128)(2,1)} %broadcast_in_dim.30), calls=%async_computation.5 | async-start | bytes 2097152 | tf_op jit(solution)/shard_map/all_to_all | solution.py:26
  164.7 1.2 copy-start
  165.9 1.0 copy-start.1
  167.0 1.0 copy-start.2
Sparse Core Ops, SparseCore 0:
  26.9 38.6 all-gather.4
  83.9 39.1 reduce-scatter.1
  125.3 33.6 all-gather.6

commit v5 on v4

--- a/solution.py
+++ b/solution.py
@@ -84,7 +84,7 @@
             jax.ShapeDtypeStruct(master.shape, jnp.float32),
             jax.ShapeDtypeStruct((groups * rows, columns), jnp.bfloat16),
         ],
-        compiler_params=pltpu.CompilerParams(vmem_limit_bytes=24 * 1024 * 1024),
+        compiler_params=pltpu.CompilerParams(vmem_limit_bytes=50 * 1024 * 1024),
         cost_estimate=pl.CostEstimate(flops=4_000_000, bytes_accessed=8_000_000, transcendentals=0),
         name="finish",
     )(h.reshape(1), source, place, own, other, pulled, master, momentum)

time: 179 us -> 177 us (0.989)
  local copies, waits for them, and re-layouts: 15.4 us -> 12.4 us
    unnamed x17 -> x13, local copies, waits for them, and re-layouts: 5.17 us -> 1.86 us
  transfers between devices with their start and end apart: 12 -> 12, of which waited for: 10 -> 10; matrix products, arithmetic and copies ran while one was open for 10% -> 9% of each run, Pallas kernels for 0% -> 0%
where the time goes in v5:
time: 177 us; the launch traced here: 176 us
  waiting for transfers between devices  81.7 us (46%)
  starting transfers between devices  52.4 us (30%)
  between operations  14 us (8%)
  local copies, waits for them, and re-layouts  12.4 us (7%)
  other arithmetic  6.83 us (4%)
  Pallas kernels  4.69 us (3%)
  matrix products  4.13 us (2%)
    all_to_all x3, waiting for transfers between devices, spread(): lax.all_to_all(jnp.broadcast_to(block[None], (lax.axis_size(axis), *block...  28.1 us
    ppermute x4, starting transfers between devices, swap(): return lax.ppermute(block, axis, [(0, 1), (1, 0)])  27.4 us
    ppermute x4, waiting for transfers between devices, swap(): return lax.ppermute(block, axis, [(0, 1), (1, 0)])  18.1 us
    all_gather x1, waiting for transfers between devices, local(): full_own = lax.all_gather(summed, 'x', axis=0, tiled=False)  12.8 us
    all_to_all x3, starting transfers between devices, spread(): lax.all_to_all(jnp.broadcast_to(block[None], (lax.axis_size(axis), *block...  11.2 us
    all_to_all x1, starting transfers between devices, local(): lax.all_to_all(sent, ('x', 'c'), split_axis=0, concat_axis=0, tiled=True)  10.3 us
    all_to_all x1, waiting for transfers between devices, local(): part = lax.all_to_all(scaled, 'y', split_axis=0, concat_axis=0, tiled=True)  9.98 us
    reduce_scatter x1, waiting for transfers between devices, local(): lax.psum_scatter(both, ('h', 'l'), scatter_dimension=0, tiled=True)  7.24 us
  transfers between devices with their start and end apart: 12, of which 10 were waited for; matrix products, arithmetic and copies ran while one was open for 9% of the time, Pallas kernels for 0%

profile of v5, /device:TPU:1, one launch (start us, length us, event | category | flops | bytes accessed | tf_op | source)
XLA Modules:
  0.0 176.1 jit_solution(5580516537073154770)
XLA Ops:
  7.2 1.1 copy.60
  8.3 0.9 copy.51
  9.2 10.3 %all-to-all-start = ((bf16[8,16,1024]{2,1,0:T(8,128)(2,1)}), bf16[8,16,1024]{2,1,0:T(8,128)(2,1)S(1)}, u32[]{:S(2)}, u32[]{:S(2)}) async-start(bf16[8,16,1024]{2,1,0:T(8,128)(2,1)} %copy.51), calls=%async_computation | async-start | bytes 524288 | tf_op jit(solution)/shard_map/all_to_all | solution.py:108
  19.5 1.1 multiply_reduce_fusion
  20.6 5.4 %all-to-all-done = bf16[8,16,1024]{2,1,0:T(8,128)(2,1)S(1)} async-done(((bf16[8,16,1024]{2,1,0:T(8,128)(2,1)}), bf16[8,16,1024]{2,1,0:T(8,128)(2,1)S(1)}, u32[]{:S(2)}, u32[]{:S(2)}) %all-to-all-start) | async-done | bytes 262176 | tf_op jit(solution)/shard_map/all_to_all | solution.py:108
  26.0 0.7 copy-done.4
  26.8 0.1 multiply_convert_fusion.2
  26.9 0.2 reshape.53
  27.2 0.1 fusion
  27.3 0.9 reshape.54
  28.2 3.4 %all-to-all-start.1 = ((bf16[8,16,1024]{2,1,0:T(8,128)(2,1)}), bf16[8,16,1024]{2,1,0:T(8,128)(2,1)S(1)}, u32[]{:S(2)}, u32[]{:S(2)}) async-start(bf16[8,16,1024]{2,1,0:T(8,128)(2,1)} %reshape.54), calls=%async_computation.1 | async-start | bytes 524288 | tf_op jit(solution)/shard_map/all_to_all | solution.py:123
  31.7 10.0 %all-to-all-done.1 = bf16[8,16,1024]{2,1,0:T(8,128)(2,1)S(1)} async-done(((bf16[8,16,1024]{2,1,0:T(8,128)(2,1)}), bf16[8,16,1024]{2,1,0:T(8,128)(2,1)S(1)}, u32[]{:S(2)}, u32[]{:S(2)}) %all-to-all-start.1) | async-done | bytes 262176 | tf_op jit(solution)/shard_map/all_to_all | solution.py:123
  41.7 1.1 broadcast_in_dim.26
  42.8 3.5 %all-to-all-start.2 = ((bf16[4,8,16,1024]{3,2,1,0:T(8,128)(2,1)}), bf16[4,8,16,1024]{3,2,1,0:T(8,128)(2,1)S(1)}, u32[]{:S(2)}, u32[]{:S(2)}) async-start(bf16[4,8,16,1024]{3,2,1,0:T(8,128)(2,1)} %broadcast_in_dim.26), calls=%async_computation.2 | async-start | bytes 2097152 | tf_op jit(solution)/shard_map/all_to_all | solution.py:26
  46.4 9.6 %collective-permute-start = (bf16[8,128,128]{2,0,1:T(8,128)(2,1)S(1)}, bf16[8,128,128]{2,0,1:T(8,128)(2,1)S(1)}, u32[]{:S(2)}, u32[]{:S(2)}) collective-permute-start(bf16[8,128,128]{2,0,1:T(8,128)(2,1)S(1)} %fusion.1), channel_id=1, source_target_pairs={{0,64},{64,0},{1,65},{65,1},{2,66},{66,2},{3,67},{67,3},{4,68},{68... | collective-permute-start | bytes 786440 | tf_op jit(solution)/shard_map/ppermute | solution.py:32
  56.0 3.8 %collective-permute-done = bf16[8,128,128]{2,0,1:T(8,128)(2,1)S(1)} collective-permute-done((bf16[8,128,128]{2,0,1:T(8,128)(2,1)S(1)}, bf16[8,128,128]{2,0,1:T(8,128)(2,1)S(1)}, u32[]{:S(2)}, u32[]{:S(2)}) %collective-permute-start) | collective-permute-done | bytes 262176 | tf_op jit(solution)/shard_map/ppermute | solution.py:32
  59.9 0.1 copy.52
  60.0 10.5 %collective-permute-start.1 = (bf16[4,8,16,1024]{3,2,0,1:T(8,128)(2,1)S(1)}, bf16[4,8,16,1024]{3,2,0,1:T(8,128)(2,1)}, u32[]{:S(2)}, u32[]{:S(2)}) collective-permute-start(bf16[4,8,16,1024]{3,2,0,1:T(8,128)(2,1)S(1)} %copy.52), channel_id=1, source_target_pairs={{0,1},{1,0},{2,3},{3,2},{4,5},{5,4},{6,7},{7,6},{8,9},{9,8},{10,11... | collective-permute-start | bytes 3145736 | tf_op jit(solution)/shard_map/ppermute | solution.py:32
  70.5 0.7 dynamic_slice.6
  71.2 1.7 collective-permute-done.1
  72.9 1.6 select_bitcast_fusion.3
  74.5 0.1 maximum_bitcast_fusion
  74.7 2.9 %multiply_convert_fusion = bf16[512,1024]{1,0:T(8,128)(2,1)S(1)} fusion(bf16[1024,512]{1,0:T(8,128)(2,1)S(1)} %bitcast.50, bf16[1024,1024]{1,0:T(8,128)(2,1)} %bitcast.48, f32[1024]{0:T(1024)S(1)} %dynamic_slice.6), kind=kOutput, calls=%fused_computation.1 | convolution fusion | flops 1074790400 | bytes 4198400 | tf_op jit(solution)/shard_map/dot_general | solution.py:149
  77.6 2.4 %collective-permute-start.2 = (bf16[512,1024]{1,0:T(8,128)(2,1)S(1)}, bf16[512,1024]{1,0:T(8,128)(2,1)S(1)}, u32[]{:S(2)}, u32[]{:S(2)}) collective-permute-start(bf16[512,1024]{1,0:T(8,128)(2,1)S(1)} %multiply_convert_fusion), channel_id=1, source_target_pairs={{0,1},{1,0},{2,3},{3,2},{4,5},{5,4},{6,7},{7,6},{8,9},{9,8},{10,11... | collective-permute-start | bytes 3145736 | tf_op jit(solution)/shard_map/ppermute | solution.py:32
  80.0 0.1 pad_maximum_fusion.1
  80.2 1.3 multiply_convert_fusion.1
  81.4 0.9 collective-permute-done.2
  82.3 1.5 pad_maximum_fusion
  83.8 0.1 convert_bitcast_fusion
  84.1 1.9 %broadcast_in_dim.27 = bf16[4,2,8,128,128]{4,3,2,1,0:T(8,128)(2,1)} broadcast(bf16[2,8,128,128]{3,2,1,0:T(8,128)(2,1)S(1)} %copy.57), dimensions={1,2,3,4} | broadcast | bytes 2621440 | tf_op jit(solution)/shard_map/broadcast_in_dim | solution.py:27
  86.0 4.1 %all-to-all-start.3 = ((bf16[4,2,8,128,128]{4,3,2,1,0:T(8,128)(2,1)}), bf16[4,2,8,128,128]{4,3,2,1,0:T(8,128)(2,1)S(1)}, u32[]{:S(2)}, u32[]{:S(2)}) async-start(bf16[4,2,8,128,128]{4,3,2,1,0:T(8,128)(2,1)} %broadcast_in_dim.27), calls=%async_computation.4 | async-start | bytes 4194304 | tf_op jit(solution)/shard_map/all_to_all | solution.py:26
  90.2 0.7 fusion.5
  90.9 0.1 reduce_window_sum.11
  91.0 0.7 compare_bitcast_fusion
  91.7 0.2 select_reduce_fusion
  91.9 0.1 select_reduce_fusion.1.source_ref
  92.0 0.7 multiply_add_fusion.place_ref
  92.7 23.2 %all-to-all-done.3 = bf16[4,2,8,128,128]{4,3,2,1,0:T(8,128)(2,1)S(1)} async-done(((bf16[4,2,8,128,128]{4,3,2,1,0:T(8,128)(2,1)}), bf16[4,2,8,128,128]{4,3,2,1,0:T(8,128)(2,1)S(1)}, u32[]{:S(2)}, u32[]{:S(2)}) %all-to-all-start.3) | async-done | bytes 2097184 | tf_op jit(solution)/shard_map/all_to_all | solution.py:26
  115.9 7.2 %reduce-scatter.2.cloned.1.call-done = bf16[128,1024]{1,0:T(8,128)(2,1)} async-done(((bf16[1024,1024]{1,0:T(8,128)(2,1)}), bf16[128,1024]{1,0:T(8,128)(2,1)}) %reduce-scatter.2.cloned.1.call-update) | async-done | bytes 262160 | tf_op jit(solution)/shard_map/reduce_scatter | solution.py:160
  123.2 4.8 %collective-permute-start.3 = (bf16[1024,128]{0,1:T(8,128)(2,1)}, bf16[1024,128]{0,1:T(8,128)(2,1)}, u32[]{:S(2)}, u32[]{:S(2)}) collective-permute-start(bf16[1024,128]{0,1:T(8,128)(2,1)} %bitcast.57), channel_id=1, source_target_pairs={{0,64},{64,0},{1,65},{65,1},{2,66},{66,2},{3,67},{67,3},{4,68},{68... | collective-permute-start | bytes 786440 | tf_op jit(solution)/shard_map/ppermute | solution.py:32
  128.0 11.7 %collective-permute-done.3 = bf16[1024,128]{0,1:T(8,128)(2,1)} collective-permute-done((bf16[1024,128]{0,1:T(8,128)(2,1)}, bf16[1024,128]{0,1:T(8,128)(2,1)}, u32[]{:S(2)}, u32[]{:S(2)}) %collective-permute-start.3) | collective-permute-done | bytes 262176 | tf_op jit(solution)/shard_map/ppermute | solution.py:32
  139.8 1.1 copy.59
  140.9 1.1 broadcast_in_dim.30
  142.0 3.5 %all-to-all-start.4 = ((bf16[4,1024,128]{2,1,0:T(8,128)(2,1)}), bf16[4,1024,128]{2,1,0:T(8,128)(2,1)S(1)}, u32[]{:S(2)}, u32[]{:S(2)}) async-start(bf16[4,1024,128]{2,1,0:T(8,128)(2,1)} %broadcast_in_dim.30), calls=%async_computation.5 | async-start | bytes 2097152 | tf_op jit(solution)/shard_map/all_to_all | solution.py:26
  145.5 12.8 %all-gather.7.cloned.1.call-done = bf16[4096,128]{0,1:T(8,128)(2,1)} async-done(((bf16[1024,128]{0,1:T(8,128)(2,1)}), bf16[4096,128]{0,1:T(8,128)(2,1)}) %all-gather.7.cloned.1.call-update) | async-done | bytes 1048592 | tf_op jit(solution)/shard_map/all_gather | solution.py:171
  158.4 1.6 copy.58
  160.0 4.9 %all-to-all-done.4.other_ref = bf16[4,1024,128]{2,1,0:T(8,128)(2,1)S(1)} async-done(((bf16[4,1024,128]{2,1,0:T(8,128)(2,1)}), bf16[4,1024,128]{2,1,0:T(8,128)(2,1)S(1)}, u32[]{:S(2)}, u32[]{:S(2)}) %all-to-all-start.4) | async-done | bytes 1048608 | tf_op jit(solution)/shard_map/all_to_all | solution.py:26
  164.8 4.7 %finish.1 = (f32[8,16384]{1,0:T(8,128)}, f32[8,16384]{1,0:T(8,128)}, bf16[8192,128]{1,0:T(8,128)(2,1)}) custom-call(s32[1]{0:T(128)} %bitcast.h_ref, s32[8]{0:T(128)S(1)} %select_reduce_fusion.1.source_ref, s32[64]{0:T(128)S(1)} %multiply_add_fusion.place_ref, bf16[4,1024,128]{2,1,0:T(8,128)(2,1)S(1)} %bitcast.46, ...), custom_call_target="tpu_custom_call" | custom-call | flops 4000000 | bytes 8000000 | tf_op jit(solution)/shard_map/finish/pallas_call | solution.py:73
  (26 shorter events, 0.6 us)
Async XLA Ops:
  7.2 19.6 %copy-start.5 = (bf16[16,8192]{1,0:T(8,128)(2,1)S(1)}, bf16[16,8192]{1,0:T(8,128)(2,1)}, u32[]{:S(2)}) copy-start(bf16[16,8192]{1,0:T(8,128)(2,1)} %param.7) | copy-start | bytes 786436
  9.2 22.4 %copy-start.2 = (f32[1,1,8,16384]{3,2,1,0:T(8,128)S(1)}, f32[1,1,8,16384]{3,2,1,0:T(8,128)}, u32[]{:S(2)}) copy-start(f32[1,1,8,16384]{3,2,1,0:T(8,128)} %param.9) | copy-start | bytes 1572868
  9.2 22.4 %copy-start.3 = (f32[1,1,8,16384]{3,2,1,0:T(8,128)S(1)}, f32[1,1,8,16384]{3,2,1,0:T(8,128)}, u32[]{:S(2)}) copy-start(f32[1,1,8,16384]{3,2,1,0:T(8,128)} %param.10) | copy-start | bytes 1572868
  9.2 16.8 %all-to-all-start = ((bf16[8,16,1024]{2,1,0:T(8,128)(2,1)}), bf16[8,16,1024]{2,1,0:T(8,128)(2,1)S(1)}, u32[]{:S(2)}, u32[]{:S(2)}) async-start(bf16[8,16,1024]{2,1,0:T(8,128)(2,1)} %copy.51), calls=%async_computation | async-start | bytes 524288 | tf_op jit(solution)/shard_map/all_to_all | solution.py:108
  19.5 55.2 %all-gather.5.cloned.1.call-start = ((), (), s32[]{:S(2)}) async-start(), calls=%async_computation.7 | async-start | bytes 2359296 | tf_op jit(solution)/shard_map/all_gather | solution.py:109
  26.0 0.7 copy-start.4
  28.2 13.5 %all-to-all-start.1 = ((bf16[8,16,1024]{2,1,0:T(8,128)(2,1)}), bf16[8,16,1024]{2,1,0:T(8,128)(2,1)S(1)}, u32[]{:S(2)}, u32[]{:S(2)}) async-start(bf16[8,16,1024]{2,1,0:T(8,128)(2,1)} %reshape.54), calls=%async_computation.1 | async-start | bytes 524288 | tf_op jit(solution)/shard_map/all_to_all | solution.py:123
  42.8 17.1 %all-to-all-start.2 = ((bf16[4,8,16,1024]{3,2,1,0:T(8,128)(2,1)}), bf16[4,8,16,1024]{3,2,1,0:T(8,128)(2,1)S(1)}, u32[]{:S(2)}, u32[]{:S(2)}) async-start(bf16[4,8,16,1024]{3,2,1,0:T(8,128)(2,1)} %broadcast_in_dim.26), calls=%async_computation.2 | async-start | bytes 2097152 | tf_op jit(solution)/shard_map/all_to_all | solution.py:26
  46.3 76.8 %reduce-scatter.2.cloned.1.call-start = ((), (), s32[]{:S(2)}) async-start(), calls=%async_computation.6 | async-start | bytes 2359296 | tf_op jit(solution)/shard_map/reduce_scatter | solution.py:160
  46.4 13.5 %collective-permute-start = (bf16[8,128,128]{2,0,1:T(8,128)(2,1)S(1)}, bf16[8,128,128]{2,0,1:T(8,128)(2,1)S(1)}, u32[]{:S(2)}, u32[]{:S(2)}) collective-permute-start(bf16[8,128,128]{2,0,1:T(8,128)(2,1)S(1)} %fusion.1), channel_id=1, source_target_pairs={{0,64},{64,0},{1,65},{65,1},{2,66},{66,2},{3,67},{67,3},{4,68},{68... | collective-permute-start | bytes 786440 | tf_op jit(solution)/shard_map/ppermute | solution.py:32
  60.0 12.9 %collective-permute-start.1 = (bf16[4,8,16,1024]{3,2,0,1:T(8,128)(2,1)S(1)}, bf16[4,8,16,1024]{3,2,0,1:T(8,128)(2,1)}, u32[]{:S(2)}, u32[]{:S(2)}) collective-permute-start(bf16[4,8,16,1024]{3,2,0,1:T(8,128)(2,1)S(1)} %copy.52), channel_id=1, source_target_pairs={{0,1},{1,0},{2,3},{3,2},{4,5},{5,4},{6,7},{7,6},{8,9},{9,8},{10,11... | collective-permute-start | bytes 3145736 | tf_op jit(solution)/shard_map/ppermute | solution.py:32
  77.6 2.5 %copy-start.1 = (bf16[64,16,1024]{2,1,0:T(8,128)(2,1)S(1)}, bf16[64,16,1024]{2,1,0:T(8,128)(2,1)}, u32[]{:S(2)}) copy-start(bf16[64,16,1024]{2,1,0:T(8,128)(2,1)} %all-gather.5.cloned.1.call-done) | copy-start | bytes 6291460
  77.6 4.7 %collective-permute-start.2 = (bf16[512,1024]{1,0:T(8,128)(2,1)S(1)}, bf16[512,1024]{1,0:T(8,128)(2,1)S(1)}, u32[]{:S(2)}, u32[]{:S(2)}) collective-permute-start(bf16[512,1024]{1,0:T(8,128)(2,1)S(1)} %multiply_convert_fusion), channel_id=1, source_target_pairs={{0,1},{1,0},{2,3},{3,2},{4,5},{5,4},{6,7},{7,6},{8,9},{9,8},{10,11... | collective-permute-start | bytes 3145736 | tf_op jit(solution)/shard_map/ppermute | solution.py:32
  86.0 29.9 %all-to-all-start.3 = ((bf16[4,2,8,128,128]{4,3,2,1,0:T(8,128)(2,1)}), bf16[4,2,8,128,128]{4,3,2,1,0:T(8,128)(2,1)S(1)}, u32[]{:S(2)}, u32[]{:S(2)}) async-start(bf16[4,2,8,128,128]{4,3,2,1,0:T(8,128)(2,1)} %broadcast_in_dim.27), calls=%async_computation.4 | async-start | bytes 4194304 | tf_op jit(solution)/shard_map/all_to_all | solution.py:26
  90.2 68.2 %all-gather.7.cloned.1.call-start = ((), (), s32[]{:S(2)}) async-start(), calls=%async_computation.8 | async-start | bytes 1310720 | tf_op jit(solution)/shard_map/all_gather | solution.py:171
  115.9 26.1 %copy-start = (bf16[4,2,8,128,128]{4,3,2,1,0:T(8,128)(2,1)}, bf16[4,2,8,128,128]{4,3,2,1,0:T(8,128)(2,1)S(1)}, u32[]{:S(2)}) copy-start(bf16[4,2,8,128,128]{4,3,2,1,0:T(8,128)(2,1)S(1)} %all-to-all-done.3) | copy-start | bytes 6291460
  123.2 16.6 %collective-permute-start.3 = (bf16[1024,128]{0,1:T(8,128)(2,1)}, bf16[1024,128]{0,1:T(8,128)(2,1)}, u32[]{:S(2)}, u32[]{:S(2)}) collective-permute-start(bf16[1024,128]{0,1:T(8,128)(2,1)} %bitcast.57), channel_id=1, source_target_pairs={{0,64},{64,0},{1,65},{65,1},{2,66},{66,2},{3,67},{67,3},{4,68},{68... | collective-permute-start | bytes 786440 | tf_op jit(solution)/shard_map/ppermute | solution.py:32
  142.0 22.8 %all-to-all-start.4 = ((bf16[4,1024,128]{2,1,0:T(8,128)(2,1)}), bf16[4,1024,128]{2,1,0:T(8,128)(2,1)S(1)}, u32[]{:S(2)}, u32[]{:S(2)}) async-start(bf16[4,1024,128]{2,1,0:T(8,128)(2,1)} %broadcast_in_dim.30), calls=%async_computation.5 | async-start | bytes 2097152 | tf_op jit(solution)/shard_map/all_to_all | solution.py:26
Sparse Core Ops, SparseCore 0:
  26.9 38.6 all-gather.4
  83.9 39.1 reduce-scatter.1
  125.3 33.0 all-gather.6
